TPU v7x, 32 devices: a whole 2x2x4 slice. The times are simulated.
32 devices in a mesh: req: 8 (over z, y), mlp: 4 (over x, core).
Axes of the slice: x: 2, y: 2, z: 4, core: 2. Of those that a mesh axis runs over, the one named last changes fastest.
Arguments:
- queries: bfloat16 [8, 2, 16, 2, 1536], P('req', None, 'mlp'), may hold values from -64 to 64
- new_kv: bfloat16 [8, 2, 16, 2, 256], P('req', None, 'mlp'), may hold values from -9 to 9
- residual: bfloat16 [8, 2, 16, 2, 1536], P('req', None, 'mlp'), may hold values from -3 to 3
- prompt_kv: bfloat16 [8, 1024, 256], P('req'), may hold values from -9 to 9
- tail_kv: bfloat16 [8, 16, 64, 256], P('req', 'mlp'), may hold values from -9 to 9
- page_pool: bfloat16 [256, 160, 256], P(('req', 'mlp')), may hold values from -9 to 9
- page_holder: int32 [32, 8], P(('req', 'mlp')), may hold values from 0 to 7, as said below
- serve_slot: int32 [32, 8], P(('req', 'mlp')), may hold values from 0 to 7
- prompt_len: int32 [8, 2], P('req'), may hold values from 512 to 32768
- tail_len: int32 [8, 2, 16], P('req', None, 'mlp'), may hold values from 1 to 62, 496 in all within a row
- w_out: bfloat16 [1536, 1536], P('mlp'), may hold values from -0.15625 to 0.15625
- norm_mlp: float32 [1536], replicated, may hold values from 0.25 to 1.75
- w_gate: bfloat16 [1536, 4608], P(None, 'mlp'), may hold values from -0.15625 to 0.15625
- w_up: bfloat16 [1536, 4608], P(None, 'mlp'), may hold values from -0.15625 to 0.15625
- w_down: bfloat16 [4608, 1536], P('mlp'), may hold values from -0.09375 to 0.09375
- norm_final: float32 [1536], replicated, may hold values from 0.25 to 1.75
- w_score: float32 [1536], replicated, may hold values from -0.15625 to 0.15625
Outputs:
- scores: float32 [8, 2, 16, 2], P('req', None, 'mlp')
- hidden_out: bfloat16 [8, 2, 16, 2, 1536], P('req', None, 'mlp')
- tails_out: bfloat16 [8, 2, 16, 64, 256], P('req', None, 'mlp')
Inputs may be any that keep to these rules, and one draw needn't show every extreme that they name: Each row of page_holder names every req index once.
All inputs are finite; a program needn't handle non-finite values. No bound on the sum of `tail_len` on one device may be relied on, other than what follows from the above.
Results may differ from a plain program's by a relative error of at most 0.015.
Values may be sent and summed in bfloat16 or wider, within the bound.
A program may use at most 64 MiB of HBM per device.

v0:
```python
import jax
import jax.numpy as jnp
from jax import lax
from jax.sharding import PartitionSpec as P


def attend(query, fresh, window, tails, plen, tlen):
    count = query.shape[0]
    size = window.shape[-1] // 2
    q = query.reshape(count, 2, -1, size)
    scale = 1.0 / jnp.sqrt(jnp.float32(size))
    s_win = (
        jnp.einsum("sthd,kd->sthk", q, window[:, :size], preferred_element_type=jnp.float32) * scale
    )
    s_tail = (
        jnp.einsum("sthd,sjd->sthj", q, tails[..., :size], preferred_element_type=jnp.float32)
        * scale
    )
    s_new = (
        jnp.einsum("sthd,sud->sthu", q, fresh[..., :size], preferred_element_type=jnp.float32)
        * scale
    )
    tpos = tlen[:, None] + jnp.arange(2, dtype=jnp.int32)[None, :]
    kw = jnp.arange(window.shape[0], dtype=jnp.int32)[None, None, None, :]
    ok_win = (kw >= window.shape[0] - plen) & (kw > tpos[:, :, None, None])
    kt = jnp.arange(tails.shape[1], dtype=jnp.int32)[None, None, None, :]
    ok_tail = kt < tlen[:, None, None, None]
    steps = jnp.arange(2, dtype=jnp.int32)
    ok_new = steps[None, None, None, :] <= steps[None, :, None, None]
    s_win = jnp.where(ok_win, s_win, -1e30)
    s_tail = jnp.where(ok_tail, s_tail, -1e30)
    s_new = jnp.where(ok_new, s_new, -1e30)
    top = jnp.maximum(jnp.maximum(s_win.max(-1), s_tail.max(-1)), s_new.max(-1))[..., None]
    e_win = jnp.where(ok_win, jnp.exp(s_win - top), 0.0)
    e_tail = jnp.where(ok_tail, jnp.exp(s_tail - top), 0.0)
    e_new = jnp.where(ok_new, jnp.exp(s_new - top), 0.0)
    total = (
        e_win.sum(-1, keepdims=True) + e_tail.sum(-1, keepdims=True) + e_new.sum(-1, keepdims=True)
    )
    p_win = (e_win / total).astype(jnp.bfloat16)
    p_tail = (e_tail / total).astype(jnp.bfloat16)
    p_new = (e_new / total).astype(jnp.bfloat16)
    out = jnp.einsum("sthk,kd->sthd", p_win, window[:, size:], preferred_element_type=jnp.float32)
    out = out + jnp.einsum(
        "sthj,sjd->sthd", p_tail, tails[..., size:], preferred_element_type=jnp.float32
    )
    out = out + jnp.einsum(
        "sthu,sud->sthd", p_new, fresh[..., size:], preferred_element_type=jnp.float32
    )
    return out.reshape(count, 2, -1).astype(jnp.bfloat16)


def extend(tails, fresh, tlen):
    rows = jnp.arange(tails.shape[1], dtype=jnp.int32)[None, :, None]
    lead = tlen[:, None, None]
    out = jnp.where(rows == lead, fresh[:, 0][:, None, :], tails)
    return jnp.where(rows == lead + 1, fresh[:, 1][:, None, :], out)


def rms_scale(values):
    return values * lax.rsqrt(jnp.mean(values * values, axis=-1, keepdims=True) + 1e-06)


def on_device(
    queries,
    new_kv,
    residual,
    prompt_kv,
    tail_kv,
    page_pool,
    page_holder,
    serve_slot,
    prompt_len,
    tail_len,
    w_out,
    norm_mlp,
    w_gate,
    w_up,
    w_down,
    norm_final,
    w_score,
):
    samp_dev = queries.shape[2]
    width = residual.shape[-1]
    kv_width = new_kv.shape[-1]
    win_rows = prompt_kv.shape[1]
    tail_rows = tail_kv.shape[2]
    outgoing = jnp.take(page_pool, serve_slot[0], axis=0)
    arrived = lax.all_to_all(outgoing, "req", split_axis=0, concat_axis=0, tiled=True)
    fetched = jnp.take(arrived, page_holder[0], axis=0).reshape(-1, kv_width)
    moved_window = fetched[:win_rows]
    moved_tails = fetched[win_rows:].reshape(samp_dev, tail_rows, kv_width)
    first = attend(
        queries[0, 0], new_kv[0, 0], prompt_kv[0], tail_kv[0], prompt_len[0, 0], tail_len[0, 0]
    )
    second = attend(
        queries[0, 1], new_kv[0, 1], moved_window, moved_tails, prompt_len[0, 1], tail_len[0, 1]
    )
    attn = jnp.stack([first, second])[None]
    tails_out = jnp.stack(
        [
            extend(tail_kv[0], new_kv[0, 0], tail_len[0, 0]),
            extend(moved_tails, new_kv[0, 1], tail_len[0, 1]),
        ]
    )[None]
    block_width = w_out.shape[0]
    position = lax.axis_index("mlp")
    every = lax.all_gather(attn, "mlp", axis=2, tiled=True)
    block = lax.dynamic_slice_in_dim(every, position * block_width, block_width, 4)
    partial_sum = jnp.dot(block.reshape(-1, block_width), w_out, preferred_element_type=jnp.float32)
    mixed = lax.psum(partial_sum, "mlp")
    res_all = lax.all_gather(residual, "mlp", axis=2, tiled=True).reshape(-1, width)
    h1_all = (res_all.astype(jnp.float32) + mixed).astype(jnp.bfloat16)
    h1_own = lax.dynamic_slice_in_dim(
        h1_all.reshape(2, -1, 2, width), position * samp_dev, samp_dev, 1
    )
    normed = (rms_scale(h1_all.astype(jnp.float32)) * norm_mlp).astype(jnp.bfloat16)
    gate = jnp.dot(normed, w_gate, preferred_element_type=jnp.float32)
    up = jnp.dot(normed, w_up, preferred_element_type=jnp.float32)
    act = (jax.nn.gelu(gate, approximate=True) * up).astype(jnp.bfloat16)
    down_terms = jnp.dot(act, w_down, preferred_element_type=jnp.float32).reshape(2, -1, 2, width)
    down_own = lax.psum_scatter(
        down_terms.astype(jnp.bfloat16), "mlp", scatter_dimension=1, tiled=True
    ).astype(jnp.float32)
    h2 = h1_own.astype(jnp.float32) + down_own
    scores = jnp.sum(rms_scale(h2) * norm_final * w_score, axis=-1)
    return (scores[None], h2.astype(jnp.bfloat16)[None], tails_out)


def solution(mesh):
    placed = (
        P("req", None, "mlp", None, None),
        P("req", None, "mlp", None, None),
        P("req", None, "mlp", None, None),
        P("req", None, None),
        P("req", "mlp", None, None),
        P(("req", "mlp"), None, None),
        P(("req", "mlp"), None),
        P(("req", "mlp"), None),
        P("req", None),
        P("req", None, "mlp"),
        P("mlp", None),
        P(),
        P(None, "mlp"),
        P(None, "mlp"),
        P("mlp", None),
        P(),
        P(),
    )
    return jax.shard_map(
        on_device,
        mesh=mesh,
        in_specs=placed,
        out_specs=(
            P("req", None, "mlp", None),
            P("req", None, "mlp", None, None),
            P("req", None, "mlp", None, None),
        ),
        check_vma=False,
    )
```

profile of v0, /device:TPU:0, one launch (start us, length us, event | category | flops | bytes accessed | tf_op | source)
XLA Modules:
  0.0 187.1 jit_solution(8959606269407668543)
XLA Ops:
  7.2 0.8 compare_select_fusion.1
  8.0 1.3 compare_and_fusion.3
  9.4 2.5 %gather_fusion = bf16[8,160,256]{2,1,0:T(8,128)(2,1)} fusion(bf16[8,160,256]{2,1,0:T(8,128)(2,1)} %param.24, s32[1024]{0:T(1024)S(1)} %pad_clamp_fusion.1), kind=kCustom, calls=%fused_computation.clone | custom fusion | bytes 1310752 | tf_op jit(solution)/shard_map/jit(_take)/gather | solution.py:88
  11.9 2.1 %broadcast_select_fusion.1 = bf16[8,160,256]{2,1,0:T(8,128)(2,1)} fusion(bf16[8,160,256]{2,1,0:T(8,128)(2,1)} %gather_fusion, pred[8]{0:T(512)(128)(4,1)} %compare_and_fusion.3), kind=kLoop, calls=%fused_computation.26 | loop fusion | flops 327680 | bytes 1310728 | tf_op jit(solution)/shard_map/jit(_take)/select_n | solution.py:88
  14.0 7.3 %all-to-all-start = ((bf16[8,160,256]{2,1,0:T(8,128)(2,1)}), bf16[8,160,256]{2,1,0:T(8,128)(2,1)}, u32[]{:S(2)}, u32[]{:S(2)}) async-start(bf16[8,160,256]{2,1,0:T(8,128)(2,1)} %broadcast_select_fusion.1), calls=%async_computation | async-start | bytes 1310720 | tf_op jit(solution)/shard_map/all_to_all | solution.py:89
  21.9 1.2 compare_and_fusion.2
  24.9 0.7 iota_compare_fusion.2
  26.2 1.4 fusion.62
  27.6 1.3 fusion.65
  30.7 1.4 reshape_squeeze.6
  32.7 1.1 fusion.68
  33.9 1.6 fusion.66
  35.4 0.8 compare_and_fusion.1
  36.2 1.3 fusion.67
  37.5 1.5 fusion.32
  39.0 0.9 fusion.11
  39.9 1.4 fusion.63
  41.3 7.1 %all_gather.6 = bf16[1,2,16,2,1536]{4,3,2,1,0:T(2,128)(2,1)} all-gather(bf16[1,2,4,2,1536]{4,3,2,1,0:T(2,128)(2,1)} %param.21), channel_id=1, replica_groups=mesh['req'=8,'mlp'=4] {'mlp'}, dimensions={2}, use_global_device_ids=true | all-gather | bytes 245760 | tf_op jit(solution)/shard_map/all_gather | solution.py:112
  48.4 1.4 reshape_squeeze.7
  49.8 1.7 reshape.390
  51.5 1.3 copy.43
  52.8 1.3 copy.44
  54.0 1.3 copy.45
  55.3 1.3 copy.46
  56.6 1.2 dynamic-slice.1
  58.5 1.3 iota_compare_fusion.3
  59.8 0.7 iota_add_fusion
  60.4 1.3 compare_and_fusion
  61.8 2.1 %fusion.69 = (f32[4,2,12]{2,1,0:T(2,128)}, f32[4,2,12,2]{2,3,1,0:T(2,128)}) fusion(bf16[4,2,12,128]{3,2,1,0:T(8,128)(2,1)} %reshape_squeeze.7, bf16[4,2,256]{2,1,0:T(2,128)(2,1)} %get-tuple-element.12, pred[2,2]{1,0:T(4,128)(4,1)} %iota_compare_fusion.8), kind=kOutput, calls=%fused_computation.152 | convolution fusion | flops 49632 | bytes 36480 | tf_op jit(solution)/shard_map/sthd,sud->sthu/dot_general | solution.py:20
  63.9 1.7 select_select_fusion.1
  65.6 2.7 %gather_fusion.1 = bf16[8,160,256]{2,1,0:T(8,128)(2,1)} fusion(bf16[8,160,256]{2,1,0:T(8,128)(2,1)} %all-to-all-done, s32[1024]{0:T(1024)} %pad_clamp_fusion), kind=kCustom, calls=%fused_computation.1.clone | custom fusion | bytes 1310752 | tf_op jit(solution)/shard_map/jit(_take)/gather | solution.py:90
  68.3 1.3 broadcast_select_fusion
  69.6 0.8 copy-done.3
  70.4 1.8 fusion.70
  72.3 1.5 fusion.71
  73.8 0.7 maximum_maximum_fusion
  75.0 1.4 fusion.50
  76.5 0.7 add_add_fusion.1
  77.1 1.4 fusion.25
  78.9 0.9 fusion.7
  79.8 1.4 convert_element_type.83
  81.1 1.0 fusion.33
  82.2 1.3 fusion.12
  83.5 0.7 add_add_fusion
  84.2 1.5 fusion.24
  85.6 1.1 convolution_add_fusion.1
  86.7 1.6 fusion.8
  88.3 1.4 convert_element_type.88
  89.7 0.8 pad_maximum_fusion
  90.5 5.6 %all-gather = bf16[2,16,2,1536]{3,2,1,0:T(2,128)(2,1)S(1)} all-gather(bf16[2,4,2,1536]{3,2,1,0:T(2,128)(2,1)S(1)} %pad_maximum_fusion), channel_id=2, replica_groups=mesh['req'=8,'mlp'=4] {'mlp'}, dimensions={1}, use_global_device_ids=true | all-gather | bytes 245760 | tf_op jit(solution)/shard_map/all_gather | solution.py:108
  96.8 1.4 reshape.387
  98.2 2.4 %fusion.72 = f32[64,1536]{1,0:T(8,128)} fusion(bf16[64,384]{1,0:T(8,128)(2,1)} %reshape.387, bf16[384,1536]{1,0:T(8,128)(2,1)} %param.29), kind=kOutput, calls=%fused_computation.155 | convolution fusion | flops 75497472 | bytes 1622016 | tf_op jit(solution)/shard_map/dot_general | solution.py:110
  100.7 1.7 select_select_fusion
  102.4 31.5 %all-reduce.4.cloned.1.call-done = f32[64,1536]{1,0:T(8,128)} async-done(((f32[64,1536]{1,0:T(8,128)}), f32[64,1536]{1,0:T(8,128)}) %all-reduce.4.cloned.1.call-update) | async-done | bytes 393232 | tf_op jit(solution)/shard_map/psum | solution.py:111
  133.9 1.3 fusion.13
  135.9 3.5 %fusion.36 = f32[64,1152]{1,0:T(8,128)} fusion(bf16[1536,1152]{1,0:T(8,128)(2,1)} %param.31, bf16[64,1536]{1,0:T(8,128)(2,1)S(1)} %get-tuple-element.7, f32[1536]{0:T(1024)S(1)} %copy-done.15, f32[64]{0:T(128)S(1)} %add_rsqrt_fusion.1), kind=kOutput, calls=%fused_computation.77 | convolution fusion | flops 226885632 | bytes 4036864 | tf_op jit(solution)/shard_map/dot_general | solution.py:118
  139.4 4.2 %convolution_convert_fusion = bf16[64,1536]{1,0:T(8,128)(2,1)} fusion(bf16[1152,1536]{1,0:T(8,128)(2,1)S(1)} %copy-done, bf16[1536,1152]{1,0:T(8,128)(2,1)} %param.32, f32[64,1152]{1,0:T(8,128)} %fusion.36, bf16[64,1536]{1,0:T(8,128)(2,1)} %copy-done.1, f32[1536]{0:T(1024)S(1)} %copy-done.15, f32[64]{0:T(128)S(1)} %add_rsqrt_fusion.1), kind=kOutput, calls=%fused_computation.4 | convolution fusion | flops 454213632 | bytes 7772416 | tf_op jit(solution)/shard_map/dot_general | solution.py:121
  143.5 1.7 convert_element_type.95
  145.2 1.7 maximum_bitcast_fusion
  146.9 1.7 reshape.388
  148.6 28.5 %all-reduce.6.cloned.1.call-done = bf16[2,16,2,1536]{3,2,1,0:T(2,128)(2,1)} async-done(((bf16[2,16,2,1536]{3,2,1,0:T(2,128)(2,1)}), bf16[2,16,2,1536]{3,2,1,0:T(2,128)(2,1)}) %all-reduce.6.cloned.1.call-update) | async-done | bytes 196624
  177.1 1.0 multiply_reduce_fusion.1
  178.1 1.5 fusion.39
  179.6 0.7 copy.20
  (66 shorter events, 6.6 us)
Async XLA Ops:
  7.2 132.2 %copy-start = (bf16[1152,1536]{1,0:T(8,128)(2,1)S(1)}, bf16[1152,1536]{1,0:T(8,128)(2,1)}, u32[]{:S(2)}) copy-start(bf16[1152,1536]{1,0:T(8,128)(2,1)} %param.33) | copy-start | bytes 10616836
  7.2 16.5 %copy-start.21 = (s32[1,2,4]{2,1,0:T(2,128)S(1)}, s32[1,2,4]{2,1,0:T(2,128)}, u32[]{:S(2)}) copy-start(s32[1,2,4]{2,1,0:T(2,128)} %param.28) | copy-start | bytes 100
  7.2 22.9 %copy-start.16 = (bf16[1,2,4,2,256]{4,3,2,1,0:T(2,128)(2,1)S(1)}, bf16[1,2,4,2,256]{4,3,2,1,0:T(2,128)(2,1)}, u32[]{:S(2)}) copy-start(bf16[1,2,4,2,256]{4,3,2,1,0:T(2,128)(2,1)} %param.20) | copy-start | bytes 24580
  14.0 51.7 %all-to-all-start = ((bf16[8,160,256]{2,1,0:T(8,128)(2,1)}), bf16[8,160,256]{2,1,0:T(8,128)(2,1)}, u32[]{:S(2)}, u32[]{:S(2)}) async-start(bf16[8,160,256]{2,1,0:T(8,128)(2,1)} %broadcast_select_fusion.1), calls=%async_computation | async-start | bytes 1310720 | tf_op jit(solution)/shard_map/all_to_all | solution.py:89
  21.2 112.7 %all-reduce.4.cloned.1.call-start = ((), (), s32[]{:S(2)}) async-start(), calls=%async_computation.1 | async-start | bytes 786432 | tf_op jit(solution)/shard_map/psum | solution.py:111
  23.7 7.0 %copy-start.20 = (s32[4]{0:T(128)}, s32[4]{0:T(128)S(1)}, u32[]{:S(2)}) copy-start(s32[4]{0:T(128)S(1)} %get-tuple-element.21) | copy-start | bytes 52
  25.6 8.3 %copy-start.18 = (pred[4,64]{1,0:T(4,128)(4,1)}, pred[4,64]{1,0:T(4,128)(4,1)S(1)}, u32[]{:S(2)}) copy-start(pred[4,64]{1,0:T(4,128)(4,1)S(1)} %get-tuple-element.40) | copy-start | bytes 772
  30.7 3.1 %copy-start.13 = (bf16[4,2,256]{2,1,0:T(2,128)(2,1)}, bf16[4,2,256]{2,1,0:T(2,128)(2,1)S(1)}, u32[]{:S(2)}) copy-start(bf16[4,2,256]{2,1,0:T(2,128)(2,1)S(1)} %get-tuple-element.13) | copy-start | bytes 12292
  33.8 6.0 %copy-start.6 = (f32[4,2,12,64]{3,2,1,0:T(8,128)}, f32[4,2,12,64]{3,2,1,0:T(8,128)S(1)}, u32[]{:S(2)}) copy-start(f32[4,2,12,64]{3,2,1,0:T(8,128)S(1)} %get-tuple-element.33) | copy-start | bytes 73732
  37.5 1.5 copy-start.2
  37.5 2.3 %copy-start.8 = (f32[1,8,12]{2,1,0:T(8,128)}, f32[1,8,12]{2,1,0:T(8,128)S(1)}, u32[]{:S(2)}) copy-start(f32[1,8,12]{2,1,0:T(8,128)S(1)} %maximum_maximum_fusion.1) | copy-start | bytes 1156
  68.3 10.3 %copy-start.5 = (bf16[1,4,64,256]{3,2,1,0:T(8,128)(2,1)S(1)}, bf16[1,4,64,256]{3,2,1,0:T(8,128)(2,1)}, u32[]{:S(2)}) copy-start(bf16[1,4,64,256]{3,2,1,0:T(8,128)(2,1)} %param.23) | copy-start | bytes 393220
  68.3 10.3 %copy-start.7 = (f32[4,2,12,64]{3,2,1,0:T(8,128)S(1)}, f32[4,2,12,64]{3,2,1,0:T(8,128)}, u32[]{:S(2)}) copy-start(f32[4,2,12,64]{3,2,1,0:T(8,128)} %copy-done.6) | copy-start | bytes 73732
  68.3 10.3 %copy-start.9 = (f32[1,8,12]{2,1,0:T(8,128)S(1)}, f32[1,8,12]{2,1,0:T(8,128)}, u32[]{:S(2)}) copy-start(f32[1,8,12]{2,1,0:T(8,128)} %copy-done.8) | copy-start | bytes 1156
  68.3 10.3 %copy-start.19 = (pred[4,64]{1,0:T(4,128)(4,1)S(1)}, pred[4,64]{1,0:T(4,128)(4,1)}, u32[]{:S(2)}) copy-start(pred[4,64]{1,0:T(4,128)(4,1)} %copy-done.18) | copy-start | bytes 772
  68.3 10.6 %copy-start.14 = (bf16[4,2,256]{2,1,0:T(2,128)(2,1)S(1)}, bf16[4,2,256]{2,1,0:T(2,128)(2,1)}, u32[]{:S(2)}) copy-start(bf16[4,2,256]{2,1,0:T(2,128)(2,1)} %copy-done.13) | copy-start | bytes 12292
  68.3 10.6 %copy-start.17 = (f32[4,2,12,2]{2,3,1,0:T(2,128)S(1)}, f32[4,2,12,2]{2,3,1,0:T(2,128)}, u32[]{:S(2)}) copy-start(f32[4,2,12,2]{2,3,1,0:T(2,128)} %get-tuple-element.29) | copy-start | bytes 2308
  68.3 10.6 %copy-start.22 = (pred[2,2]{1,0:T(4,128)(4,1)S(1)}, pred[2,2]{1,0:T(4,128)(4,1)}, u32[]{:S(2)}) copy-start(pred[2,2]{1,0:T(4,128)(4,1)} %iota_compare_fusion.8) | copy-start | bytes 16
  69.6 0.8 copy-start.3
  70.4 1.8 copy-start.4
  74.5 0.6 copy-start.10
  78.6 7.0 %copy-start.11 = (f32[1,8,12]{2,1,0:T(8,128)S(1)}, f32[1,8,12]{2,1,0:T(8,128)}, u32[]{:S(2)}) copy-start(f32[1,8,12]{2,1,0:T(8,128)} %copy-done.10) | copy-start | bytes 1156
  78.6 8.1 %copy-start.12 = (bf16[4,2,256]{2,1,0:T(2,128)(2,1)S(1)}, bf16[4,2,256]{2,1,0:T(2,128)(2,1)}, u32[]{:S(2)}) copy-start(bf16[4,2,256]{2,1,0:T(2,128)(2,1)} %get-tuple-element.12) | copy-start | bytes 12292
  84.2 51.7 %copy-start.15 = (f32[1536]{0:T(1024)S(1)}, f32[1536]{0:T(1024)}, u32[]{:S(2)}) copy-start(f32[1536]{0:T(1024)} %param.30) | copy-start | bytes 18436
  100.6 76.5 %all-reduce.6.cloned.1.call-start = ((), (), s32[]{:S(2)}) async-start(), calls=%async_computation.2 | async-start | bytes 393216
  135.2 0.7 copy-start.1
Sparse Core Ops, SparseCore 0:
  100.8 33.1 all-reduce.3
  145.4 31.7 all-reduce.5
where the time goes:
time: 189 us; the launch traced here: 187 us
  waiting for transfers between devices  60 us (32%)
  other arithmetic  32.9 us (17%)
  local copies, waits for them, and re-layouts  31.7 us (17%)
  matrix products  26.1 us (14%)
  between operations  16.3 us (9%)
  blocking collectives  12.8 us (7%)
  starting transfers between devices  7.36 us (4%)
    psum x1, waiting for transfers between devices, on_device(): mixed = lax.psum(partial_sum, 'mlp')  31.5 us
    unnamed x3, waiting for transfers between devices  28.5 us
    unnamed x52, local copies, waits for them, and re-layouts  9.09 us
    all_to_all x1, starting transfers between devices, on_device(): lax.all_to_all(outgoing, 'req', split_axis=0, concat_axis=0, tiled=True)  7.28 us
    all_gather x1, blocking collectives, on_device(): lax.all_gather(residual, 'mlp', axis=2, tiled=True).reshape(-1, width)  7.15 us
    all_gather x1, blocking collectives, on_device(): every = lax.all_gather(attn, 'mlp', axis=2, tiled=True)  5.61 us
    dot_general x1, matrix products, on_device(): jnp.dot(act, w_down, preferred_element_type=jnp.float32)  4.17 us
  transfers between devices with their start and end apart: 3, of which 2 were waited for; matrix products, arithmetic and copies ran while one was open for 21% of the time, Pallas kernels for 0%

commit v1 on v0

v1 whole, which is shorter than its diff:
```python
import functools

import jax
import jax.numpy as jnp
from jax import lax
from jax.experimental import pallas as pl
from jax.experimental.pallas import tpu as pltpu
from jax.sharding import PartitionSpec as P

F32 = jnp.float32
BF16 = jnp.bfloat16
MESH = pl.DeviceIdType.MESH
HEAD = 128
LANES = 128


def page_order(count):
    half = count // 2
    return sorted(range(1, count), key=lambda d: (abs(d - half), d))


def block_kernel(
    n_req,
    n_mlp,
    exchange,
    holder_ref,
    slot_ref,
    plen_ref,
    tlen_ref,
    q_ref,
    new_ref,
    res_ref,
    norm_mlp_ref,
    norm_final_ref,
    w_score_ref,
    pool_hbm,
    prompt_hbm,
    tail_hbm,
    w_out_hbm,
    w_gate_hbm,
    w_up_hbm,
    w_down_hbm,
    scores_ref,
    hidden_ref,
    tails_ref,
    pool,
    outgoing,
    arrived,
    kv,
    w_out,
    w_gate,
    w_up,
    w_down,
    qf,
    nf,
    rf,
    attn_send,
    attn_recv,
    mix_own,
    mix_send,
    mix_recv,
    normed,
    down_own,
    down_send,
    down_recv,
    h1_own,
    load_sem,
    page_send_sem,
    page_recv_sem,
    mlp_send_sem,
    mlp_recv_sem,
):
    samp = q_ref.shape[2]
    width = res_ref.shape[-1]
    rows = 2 * samp * 2
    half = samp * 2
    win = prompt_hbm.shape[0]
    tail_rows = tails_ref.shape[3]
    fetched_rows = win + samp * tail_rows
    kv_rows = kv.shape[1]
    heads = q_ref.shape[-1] // HEAD
    block = w_out_hbm.shape[0]
    hidden = w_gate_hbm.shape[1]
    r = lax.axis_index("req")
    m = lax.axis_index("mlp")

    barrier = pltpu.get_barrier_semaphore()
    peers = n_mlp - 1
    for d in range(1, n_mlp):
        pl.semaphore_signal(
            barrier, inc=1, device_id={"mlp": lax.rem(m + d, n_mlp)}, device_id_type=MESH
        )
    if exchange:
        peers += n_req - 1
        for d in range(1, n_req):
            pl.semaphore_signal(
                barrier, inc=1, device_id={"req": lax.rem(r + d, n_req)}, device_id_type=MESH
            )

    loads = []

    def load(src, dst):
        copy = pltpu.make_async_copy(src, dst, load_sem.at[len(loads)])
        copy.start()
        loads.append(copy)
        return copy

    pool_load = load(pool_hbm, pool) if exchange else load(pool_hbm, kv.at[1, 0:fetched_rows])
    prompt_load = load(prompt_hbm, kv.at[0, 0:win])
    tail_load = load(tail_hbm, kv.at[0, win:fetched_rows])
    w_out_load = load(w_out_hbm, w_out)
    w_gate_load = load(w_gate_hbm, w_gate)
    w_up_load = load(w_up_hbm, w_up)
    w_down_load = load(w_down_hbm, w_down)

    pages = []
    if exchange:
        page = pool.shape[1]
        pool_load.wait()
        for d in page_order(n_req):
            target = lax.rem(r + d, n_req)
            outgoing[target] = pool[slot_ref[0, target]]
        pl.semaphore_wait(barrier, peers)
        for d in page_order(n_req):
            target = lax.rem(r + d, n_req)
            copy = pltpu.make_async_remote_copy(
                src_ref=outgoing.at[target],
                dst_ref=arrived.at[r],
                send_sem=page_send_sem.at[d],
                recv_sem=page_recv_sem.at[d],
                device_id={"req": target},
                device_id_type=MESH,
            )
            copy.start()
            pages.append(copy)
        arrived[r] = pool[slot_ref[0, r]]
    else:
        pl.semaphore_wait(barrier, peers)

    for i in range(2 * samp):
        q, s = divmod(i, samp)
        qf[2 * i : 2 * i + 2, :] = q_ref[0, q, s].astype(F32)
        nf[2 * i : 2 * i + 2, :] = new_ref[0, q, s].astype(F32)
        rf[2 * i : 2 * i + 2, :] = res_ref[0, q, s].astype(F32)
    fresh = jnp.concatenate(
        [nf[...], jnp.zeros((kv_rows - fetched_rows - rows, nf.shape[1]), F32)], axis=0
    ).astype(BF16)
    kv[0, fetched_rows:kv_rows, :] = fresh
    kv[1, fetched_rows:kv_rows, :] = fresh

    def attend(q):
        own = qf[q * half : (q + 1) * half, :]
        query = jnp.concatenate(
            [own[:, h * HEAD : (h + 1) * HEAD] for h in range(heads)], axis=0
        ).astype(BF16)
        count = heads * half
        scores = lax.dot_general(
            query,
            kv[q, :, 0:HEAD],
            (((1,), (1,)), ((), ())),
            preferred_element_type=F32,
        ) * (1.0 / jnp.sqrt(F32(HEAD)))
        line = lax.broadcasted_iota(jnp.int32, (count, 1), 0) % half
        token = line % 2
        sample = line // 2
        length = jnp.zeros((count, 1), jnp.int32)
        for s in range(samp):
            length = jnp.where(sample == s, tlen_ref[0, q, s], length)
        first = jnp.maximum(win - plen_ref[0, q], length + token + 1)
        col = lax.broadcasted_iota(jnp.int32, (1, win), 1)
        s_win = jnp.where(col >= first, scores[:, 0:win], -1e30)
        col = lax.broadcasted_iota(jnp.int32, (1, samp * tail_rows), 1)
        place = col - sample * tail_rows
        s_tail = jnp.where(
            (place >= 0) & (place < length), scores[:, win:fetched_rows], -1e30
        )
        col = lax.broadcasted_iota(jnp.int32, (1, kv_rows - fetched_rows), 1)
        place = col - (q * half + sample * 2)
        s_new = jnp.where(
            (place >= 0) & (place <= token), scores[:, fetched_rows:kv_rows], -1e30
        )
        scores = jnp.concatenate([s_win, s_tail, s_new], axis=1)
        top = jnp.max(scores, axis=1, keepdims=True)
        e = jnp.exp(scores - top)
        total = jnp.sum(e, axis=1, keepdims=True)
        out = jnp.dot(e.astype(BF16), kv[q, :, HEAD : 2 * HEAD], preferred_element_type=F32)
        return out / total

    def write_tails(q):
        line = lax.broadcasted_iota(jnp.int32, (tail_rows, 1), 0)
        for s in range(samp):
            i = (q * samp + s) * 2
            lead = tlen_ref[0, q, s]
            old = kv[q, win + s * tail_rows : win + (s + 1) * tail_rows, :].astype(F32)
            out = jnp.where(line == lead, nf[i : i + 1, :], old)
            out = jnp.where(line == lead + 1, nf[i + 1 : i + 2, :], out)
            tails_ref[0, q, s] = out.astype(BF16)

    prompt_load.wait()
    tail_load.wait()
    first = attend(0)
    write_tails(0)

    if exchange:
        for copy in pages:
            copy.wait_recv()
        for p in range(n_req):
            kv[1, p * page : (p + 1) * page, :] = arrived[holder_ref[0, p]]
    else:
        pool_load.wait()
    second = attend(1)

    def pieces(out, j):
        per = block // HEAD
        return jnp.concatenate(
            [out[(j * per + h) * half : (j * per + h + 1) * half, :] for h in range(per)], axis=1
        )

    for j in range(n_mlp):
        attn_send[j] = jnp.concatenate([pieces(first, j), pieces(second, j)], axis=0).astype(BF16)

    def send_all(phase, source, place):
        copies = []
        for d in range(1, n_mlp):
            target = lax.rem(m + d, n_mlp)
            copy = pltpu.make_async_remote_copy(
                src_ref=source(target),
                dst_ref=place(d),
                send_sem=mlp_send_sem.at[phase, d],
                recv_sem=mlp_recv_sem.at[phase, d],
                device_id={"mlp": target},
                device_id_type=MESH,
            )
            copy.start()
            copies.append(copy)
        return copies

    gathered = send_all(0, lambda t: attn_send.at[t], lambda d: attn_recv.at[m])
    attn_recv[m] = attn_send[m]
    write_tails(1)
    w_out_load.wait()
    for copy in gathered:
        copy.wait_recv()
    every = jnp.concatenate([attn_recv[j] for j in range(n_mlp)], axis=0)
    mixed = jnp.dot(every, w_out[...], preferred_element_type=F32)
    for j in range(n_mlp):
        part = mixed[j * rows : (j + 1) * rows, :]
        mix_own[j] = part
        mix_send[j] = part.astype(BF16)
    summed = send_all(1, lambda t: mix_send.at[t], lambda d: mix_recv.at[d])
    total = rf[...] + mix_own[m]
    for d in range(1, n_mlp):
        summed[d - 1].wait_recv()
        total = total + mix_recv[d].astype(F32)
    h1 = total.astype(BF16).astype(F32)
    h1_own[...] = h1
    scale = lax.rsqrt(jnp.mean(h1 * h1, axis=-1, keepdims=True) + 1e-06)
    normed[m] = (h1 * scale * norm_mlp_ref[...]).astype(BF16)
    spread = send_all(2, lambda t: normed.at[m], lambda d: normed.at[m])
    w_gate_load.wait()
    w_up_load.wait()
    w_down_load.wait()
    for copy in spread:
        copy.wait_recv()
    every = jnp.concatenate([normed[j] for j in range(n_mlp)], axis=0)
    step = 3 * LANES if hidden % (3 * LANES) == 0 else hidden
    acts = []
    for c in range(0, hidden, step):
        gate = jnp.dot(every, w_gate[:, c : c + step], preferred_element_type=F32)
        up = jnp.dot(every, w_up[:, c : c + step], preferred_element_type=F32)
        acts.append((jax.nn.gelu(gate, approximate=True) * up).astype(BF16))
    act = jnp.concatenate(acts, axis=1)
    down = jnp.dot(act, w_down[...], preferred_element_type=F32)
    for j in range(n_mlp):
        part = down[j * rows : (j + 1) * rows, :]
        down_own[j] = part
        down_send[j] = part.astype(BF16)
    last = send_all(3, lambda t: down_send.at[t], lambda d: down_recv.at[d])
    h2 = h1_own[...] + down_own[m]
    for d in range(1, n_mlp):
        last[d - 1].wait_recv()
        h2 = h2 + down_recv[d].astype(F32)
    scale = lax.rsqrt(jnp.mean(h2 * h2, axis=-1, keepdims=True) + 1e-06)
    scores_ref[...] = jnp.sum(
        h2 * scale * norm_final_ref[...] * w_score_ref[...], axis=-1, keepdims=True
    )
    rf[...] = h2
    for i in range(2 * samp):
        q, s = divmod(i, samp)
        hidden_ref[0, q, s] = rf[2 * i : 2 * i + 2, :].astype(BF16)
    for copy in pages + gathered + summed + spread + last:
        copy.wait_send()


def on_device(
    n_req,
    n_mlp,
    queries,
    new_kv,
    residual,
    prompt_kv,
    tail_kv,
    page_pool,
    page_holder,
    serve_slot,
    prompt_len,
    tail_len,
    w_out,
    norm_mlp,
    w_gate,
    w_up,
    w_down,
    norm_final,
    w_score,
):
    samp = queries.shape[2]
    width = residual.shape[-1]
    kv_width = new_kv.shape[-1]
    win = prompt_kv.shape[1]
    tail_rows = tail_kv.shape[2]
    fetched_rows = win + samp * tail_rows
    page = page_pool.shape[1]
    rows = 4 * samp
    block = w_out.shape[0]
    hidden = w_gate.shape[1]
    exchange = page % 16 == 0
    if exchange:
        pool = page_pool
        page_bufs = (n_req, page, kv_width)
    else:
        outgoing = jnp.take(page_pool, serve_slot[0], axis=0)
        arrived = lax.all_to_all(outgoing, "req", split_axis=0, concat_axis=0, tiled=True)
        pool = jnp.take(arrived, page_holder[0], axis=0).reshape(-1, kv_width)
        page_bufs = (1, 16, kv_width)
    pool_buf = page_pool.shape if exchange else page_bufs
    vmem = pl.BlockSpec(memory_space=pltpu.VMEM)
    smem = pl.BlockSpec(memory_space=pltpu.SMEM)
    hbm = pl.BlockSpec(memory_space=pl.ANY)
    sems = n_req if exchange else 1
    scores, hidden_out, tails_out = pl.pallas_call(
        functools.partial(block_kernel, n_req, n_mlp, exchange),
        out_shape=(
            jax.ShapeDtypeStruct((rows, 1), F32),
            jax.ShapeDtypeStruct(residual.shape, BF16),
            jax.ShapeDtypeStruct((1, 2, samp, tail_rows, kv_width), BF16),
        ),
        in_specs=[smem] * 4 + [vmem] * 6 + [hbm] * 7,
        out_specs=(vmem, vmem, vmem),
        scratch_shapes=[
            pltpu.VMEM(pool_buf, BF16),
            pltpu.VMEM(page_bufs, BF16),
            pltpu.VMEM(page_bufs, BF16),
            pltpu.VMEM((2, fetched_rows + LANES, kv_width), BF16),
            pltpu.VMEM(w_out.shape, BF16),
            pltpu.VMEM(w_gate.shape, BF16),
            pltpu.VMEM(w_up.shape, BF16),
            pltpu.VMEM(w_down.shape, BF16),
            pltpu.VMEM((rows, queries.shape[-1]), F32),
            pltpu.VMEM((rows, kv_width), F32),
            pltpu.VMEM((rows, width), F32),
            pltpu.VMEM((n_mlp, rows, block), BF16),
            pltpu.VMEM((n_mlp, rows, block), BF16),
            pltpu.VMEM((n_mlp, rows, width), F32),
            pltpu.VMEM((n_mlp, rows, width), BF16),
            pltpu.VMEM((n_mlp, rows, width), BF16),
            pltpu.VMEM((n_mlp, rows, width), BF16),
            pltpu.VMEM((n_mlp, rows, width), F32),
            pltpu.VMEM((n_mlp, rows, width), BF16),
            pltpu.VMEM((n_mlp, rows, width), BF16),
            pltpu.VMEM((rows, width), F32),
            pltpu.SemaphoreType.DMA((7,)),
            pltpu.SemaphoreType.DMA((sems,)),
            pltpu.SemaphoreType.DMA((sems,)),
            pltpu.SemaphoreType.DMA((4, n_mlp)),
            pltpu.SemaphoreType.DMA((4, n_mlp)),
        ],
        compiler_params=pltpu.CompilerParams(
            collective_id=0, has_side_effects=True, vmem_limit_bytes=48 * 1024 * 1024
        ),
        cost_estimate=pl.CostEstimate(
            flops=2 * n_mlp * rows * width * (block + 3 * hidden),
            bytes_accessed=2 * width * (block + 3 * hidden),
            transcendentals=0,
        ),
    )(
        page_holder,
        serve_slot,
        prompt_len,
        tail_len,
        queries,
        new_kv,
        residual,
        norm_mlp.reshape(1, -1),
        norm_final.reshape(1, -1),
        w_score.reshape(1, -1),
        pool,
        prompt_kv.reshape(win, kv_width),
        tail_kv.reshape(samp * tail_rows, kv_width),
        w_out,
        w_gate,
        w_up,
        w_down,
    )
    return scores.reshape(1, 2, samp, 2), hidden_out, tails_out


def solution(mesh):
    placed = (
        P("req", None, "mlp", None, None),
        P("req", None, "mlp", None, None),
        P("req", None, "mlp", None, None),
        P("req", None, None),
        P("req", "mlp", None, None),
        P(("req", "mlp"), None, None),
        P(("req", "mlp"), None),
        P(("req", "mlp"), None),
        P("req", None),
        P("req", None, "mlp"),
        P("mlp", None),
        P(),
        P(None, "mlp"),
        P(None, "mlp"),
        P("mlp", None),
        P(),
        P(),
    )
    return jax.shard_map(
        functools.partial(on_device, mesh.shape["req"], mesh.shape["mlp"]),
        mesh=mesh,
        in_specs=placed,
        out_specs=(
            P("req", None, "mlp", None),
            P("req", None, "mlp", None, None),
            P("req", None, "mlp", None, None),
        ),
        check_vma=False,
    )
```

time: 189 us -> 51.9 us (0.27)
  waiting for transfers between devices: 60 us -> 0 us
  Pallas kernels: 0 us -> 36.9 us
  other arithmetic: 32.9 us -> 0.12 us
  matrix products: 26.1 us -> 0 us
  local copies, waits for them, and re-layouts: 31.7 us -> 13.4 us
  between operations: 16.3 us -> 0.65 us
  blocking collectives: 12.8 us -> 0 us
  starting transfers between devices: 7.36 us -> 0 us
    pallas_call x0 -> x1, Pallas kernels: none -> 36.9 us  [on_device(): pl.pallas_call(functools.partial(block_kernel, n_req, n_mlp, exchange), o...]
    psum x1 -> x0, waiting for transfers between devices: 31.5 us -> none  [on_device(): mixed = lax.psum(partial_sum, 'mlp')]
    unnamed x3 -> x0, waiting for transfers between devices: 28.5 us -> none
    dot_general x15 -> x0, matrix products: 26.1 us -> none  [the longest x1 4.17 us: on_device(): jnp.dot(act, w_down, preferred_element_type=jnp.float32)]
    all_gather x2 -> x0, blocking collectives: 12.8 us -> none  [the longest x1 7.15 us: on_device(): lax.all_gather(residual, 'mlp', axis=2, tiled=True).reshape(-1, width)]
    reduce_sum x7 -> x0, other arithmetic: 8.31 us -> none  [the longest x2 2.49 us: attend(): e_tail.sum(-1, keepdims=True)]
    select_n x6 -> x0, other arithmetic: 8.25 us -> none  [the longest x2 3.41 us: extend(): return jnp.where(rows == lead + 1, fresh[:, 1][:, None, :], out)]
    all_to_all x1 -> x0, starting transfers between devices: 7.28 us -> none  [on_device(): lax.all_to_all(outgoing, 'req', split_axis=0, concat_axis=0, tiled=True)]
  transfers between devices with their start and end apart: 3 -> 0, of which waited for: 2 -> 0; matrix products, arithmetic and copies ran while one was open for 21% -> 0% of each run, Pallas kernels for 0% -> 0%
where the time goes in v1:
time: 51.9 us; the launch traced here: 51.1 us
  Pallas kernels  36.9 us (71%)
  local copies, waits for them, and re-layouts  13.4 us (26%)
  between operations  0.65 us (1%)
    pallas_call x1, Pallas kernels, on_device(): pl.pallas_call(functools.partial(block_kernel, n_req, n_mlp, exchange), o...  36.9 us
    unnamed x25, local copies, waits for them, and re-layouts  11.2 us

profile of v1, /device:TPU:0, one launch (start us, length us, event | category | flops | bytes accessed | tf_op | source)
XLA Modules:
  0.0 51.1 jit_solution(547250928631189462)
XLA Ops:
  0.6 0.7 %reshape.24.norm_mlp_ref = f32[1,1536]{1,0:T(1,128)S(1)} reshape(f32[1536]{0:T(1024)} %param.28) | data formatting | bytes 12288 | tf_op jit(solution)/shard_map/reshape | solution.py:393
  1.3 0.7 %reshape.25.norm_final_ref = f32[1,1536]{1,0:T(1,128)S(1)} reshape(f32[1536]{0:T(1024)} %param.32) | data formatting | bytes 12288 | tf_op jit(solution)/shard_map/reshape | solution.py:394
  2.0 0.7 %reshape.26.w_score_ref = f32[1,1536]{1,0:T(1,128)S(1)} reshape(f32[1536]{0:T(1024)} %param.33) | data formatting | bytes 12288 | tf_op jit(solution)/shard_map/reshape | solution.py:395
  2.7 0.0 copy-start
  2.7 1.3 %copy-done = bf16[384,1536]{1,0:T(8,128)(2,1)S(1)} copy-done((bf16[384,1536]{1,0:T(8,128)(2,1)S(1)}, bf16[384,1536]{1,0:T(8,128)(2,1)}, u32[]{:S(2)}) %copy-start) | copy-done | bytes 1179672
  4.0 0.0 copy-start.1
  4.0 1.1 %copy-done.1 = bf16[8,160,256]{2,1,0:T(8,128)(2,1)S(1)} copy-done((bf16[8,160,256]{2,1,0:T(8,128)(2,1)S(1)}, bf16[8,160,256]{2,1,0:T(8,128)(2,1)}, u32[]{:S(2)}) %copy-start.1) | copy-done | bytes 655384
  5.1 0.0 copy-start.2
  5.1 1.0 %copy-done.2 = bf16[1,1024,256]{2,1,0:T(8,128)(2,1)S(1)} copy-done((bf16[1,1024,256]{2,1,0:T(8,128)(2,1)S(1)}, bf16[1,1024,256]{2,1,0:T(8,128)(2,1)}, u32[]{:S(2)}) %copy-start.2) | copy-done | bytes 524312
  6.1 0.0 copy-start.3
  6.1 0.9 %copy-done.3 = bf16[1,4,64,256]{3,2,1,0:T(8,128)(2,1)S(1)} copy-done((bf16[1,4,64,256]{3,2,1,0:T(8,128)(2,1)S(1)}, bf16[1,4,64,256]{3,2,1,0:T(8,128)(2,1)}, u32[]{:S(2)}) %copy-start.3) | copy-done | bytes 131096
  7.0 0.0 copy-start.4
  7.0 0.8 %copy-done.4 = bf16[1,2,4,2,1536]{4,3,2,1,0:T(2,128)(2,1)S(1)} copy-done((bf16[1,2,4,2,1536]{4,3,2,1,0:T(2,128)(2,1)S(1)}, bf16[1,2,4,2,1536]{4,3,2,1,0:T(2,128)(2,1)}, u32[]{:S(2)}) %copy-start.4) | copy-done | bytes 49176
  7.8 0.0 copy-start.5
  7.8 0.8 %copy-done.5 = bf16[1,2,4,2,1536]{4,3,2,1,0:T(2,128)(2,1)S(1)} copy-done((bf16[1,2,4,2,1536]{4,3,2,1,0:T(2,128)(2,1)S(1)}, bf16[1,2,4,2,1536]{4,3,2,1,0:T(2,128)(2,1)}, u32[]{:S(2)}) %copy-start.5) | copy-done | bytes 49176
  8.6 0.0 copy-start.6
  8.6 0.7 %copy-done.6 = bf16[1,2,4,2,256]{4,3,2,1,0:T(2,128)(2,1)S(1)} copy-done((bf16[1,2,4,2,256]{4,3,2,1,0:T(2,128)(2,1)S(1)}, bf16[1,2,4,2,256]{4,3,2,1,0:T(2,128)(2,1)}, u32[]{:S(2)}) %copy-start.6) | copy-done | bytes 8216
  9.3 0.0 copy-start.7
  9.3 0.7 %copy-done.7 = s32[1,2,4]{2,1,0:T(2,128)S(1)} copy-done((s32[1,2,4]{2,1,0:T(2,128)S(1)}, s32[1,2,4]{2,1,0:T(2,128)}, u32[]{:S(2)}) %copy-start.7) | copy-done | bytes 56
  10.0 0.0 copy-start.8
  10.0 0.7 %copy-done.8 = s32[1,8]{1,0:T(1,128)S(1)} copy-done((s32[1,8]{1,0:T(1,128)S(1)}, s32[1,8]{1,0:T(1,128)}, u32[]{:S(2)}) %copy-start.8) | copy-done | bytes 56
  10.7 0.0 copy-start.9
  10.7 0.7 %copy-done.9 = s32[1,8]{1,0:T(1,128)S(1)} copy-done((s32[1,8]{1,0:T(1,128)S(1)}, s32[1,8]{1,0:T(1,128)}, u32[]{:S(2)}) %copy-start.9) | copy-done | bytes 56
  11.3 0.0 copy-start.10
  11.3 0.7 %copy-done.10 = s32[1,2]{1,0:T(1,128)S(1)} copy-done((s32[1,2]{1,0:T(1,128)S(1)}, s32[1,2]{1,0:T(1,128)}, u32[]{:S(2)}) %copy-start.10) | copy-done | bytes 32
  12.0 36.9 %shard_map.184 = (f32[16,1]{1,0:T(8,128)S(1)}, bf16[1,2,4,2,1536]{4,3,2,1,0:T(2,128)(2,1)S(1)}, bf16[1,2,4,64,256]{4,3,2,1,0:T(8,128)(2,1)S(1)}) custom-call(s32[1,8]{1,0:T(1,128)S(1)} %copy-done.8, s32[1,8]{1,0:T(1,128)S(1)} %copy-done.9, s32[1,2]{1,0:T(1,128)S(1)} %copy-done.10, s32[1,2,4]{2,1,0:T(2,128)S(1)} %copy-done.7, ...), custom_call_target="tpu_custom_call" | custom-call | flops 754974720 | bytes 11796480 | tf_op jit(solution)/shard_map/pallas_call | solution.py:340
  48.9 0.1 reduce
  49.0 0.1 reshape.29
  49.1 0.7 %copy.21 = f32[1,2,4,2]{2,3,1,0:T(2,128)} copy(f32[1,2,4,2]{3,2,1,0:T(4,128)S(1)} %reshape.29) | data formatting | bytes 128
  49.7 0.6 %copy.24 = bf16[1,2,4,2,1536]{4,3,2,1,0:T(2,128)(2,1)} copy(bf16[1,2,4,2,1536]{4,3,2,1,0:T(2,128)(2,1)S(1)} %get-tuple-element.19) | data formatting | bytes 98304
  50.4 0.7 %copy.25 = bf16[1,2,4,64,256]{4,3,2,1,0:T(8,128)(2,1)} copy(bf16[1,2,4,64,256]{4,3,2,1,0:T(8,128)(2,1)S(1)} %get-tuple-element.20) | data formatting | bytes 524288
Async XLA Ops:
  2.7 1.3 %copy-start = (bf16[384,1536]{1,0:T(8,128)(2,1)S(1)}, bf16[384,1536]{1,0:T(8,128)(2,1)}, u32[]{:S(2)}) copy-start(bf16[384,1536]{1,0:T(8,128)(2,1)} %w_out_hbm.1) | copy-start | bytes 3538948
  4.0 1.1 %copy-start.1 = (bf16[8,160,256]{2,1,0:T(8,128)(2,1)S(1)}, bf16[8,160,256]{2,1,0:T(8,128)(2,1)}, u32[]{:S(2)}) copy-start(bf16[8,160,256]{2,1,0:T(8,128)(2,1)} %pool_hbm.1) | copy-start | bytes 1966084
  5.1 1.0 %copy-start.2 = (bf16[1,1024,256]{2,1,0:T(8,128)(2,1)S(1)}, bf16[1,1024,256]{2,1,0:T(8,128)(2,1)}, u32[]{:S(2)}) copy-start(bf16[1,1024,256]{2,1,0:T(8,128)(2,1)} %param.20) | copy-start | bytes 1572868
  6.1 0.9 %copy-start.3 = (bf16[1,4,64,256]{3,2,1,0:T(8,128)(2,1)S(1)}, bf16[1,4,64,256]{3,2,1,0:T(8,128)(2,1)}, u32[]{:S(2)}) copy-start(bf16[1,4,64,256]{3,2,1,0:T(8,128)(2,1)} %param.21) | copy-start | bytes 393220
  7.0 0.8 %copy-start.4 = (bf16[1,2,4,2,1536]{4,3,2,1,0:T(2,128)(2,1)S(1)}, bf16[1,2,4,2,1536]{4,3,2,1,0:T(2,128)(2,1)}, u32[]{:S(2)}) copy-start(bf16[1,2,4,2,1536]{4,3,2,1,0:T(2,128)(2,1)} %q_ref.1) | copy-start | bytes 147460
  7.8 0.8 %copy-start.5 = (bf16[1,2,4,2,1536]{4,3,2,1,0:T(2,128)(2,1)S(1)}, bf16[1,2,4,2,1536]{4,3,2,1,0:T(2,128)(2,1)}, u32[]{:S(2)}) copy-start(bf16[1,2,4,2,1536]{4,3,2,1,0:T(2,128)(2,1)} %res_ref.1) | copy-start | bytes 147460
  8.6 0.7 %copy-start.6 = (bf16[1,2,4,2,256]{4,3,2,1,0:T(2,128)(2,1)S(1)}, bf16[1,2,4,2,256]{4,3,2,1,0:T(2,128)(2,1)}, u32[]{:S(2)}) copy-start(bf16[1,2,4,2,256]{4,3,2,1,0:T(2,128)(2,1)} %new_ref.1) | copy-start | bytes 24580
  9.3 0.7 %copy-start.7 = (s32[1,2,4]{2,1,0:T(2,128)S(1)}, s32[1,2,4]{2,1,0:T(2,128)}, u32[]{:S(2)}) copy-start(s32[1,2,4]{2,1,0:T(2,128)} %tlen_ref.1) | copy-start | bytes 100
  10.0 0.7 %copy-start.8 = (s32[1,8]{1,0:T(1,128)S(1)}, s32[1,8]{1,0:T(1,128)}, u32[]{:S(2)}) copy-start(s32[1,8]{1,0:T(1,128)} %holder_ref.1) | copy-start | bytes 100
  10.7 0.7 %copy-start.9 = (s32[1,8]{1,0:T(1,128)S(1)}, s32[1,8]{1,0:T(1,128)}, u32[]{:S(2)}) copy-start(s32[1,8]{1,0:T(1,128)} %slot_ref.1) | copy-start | bytes 100
  11.3 0.7 %copy-start.10 = (s32[1,2]{1,0:T(1,128)S(1)}, s32[1,2]{1,0:T(1,128)}, u32[]{:S(2)}) copy-start(s32[1,2]{1,0:T(1,128)} %plen_ref.1) | copy-start | bytes 28

commit v2 on v1

--- a/solution.py
+++ b/solution.py
@@ -23,6 +23,26 @@
     n_req,
     n_mlp,
     exchange,
+    holder_hbm,
+    slot_hbm,
+    plen_hbm,
+    tlen_hbm,
+    q_hbm,
+    new_hbm,
+    res_hbm,
+    norm_mlp_hbm,
+    norm_final_hbm,
+    w_score_hbm,
+    pool_hbm,
+    prompt_hbm,
+    tail_hbm,
+    w_out_hbm,
+    w_gate_hbm,
+    w_up_hbm,
+    w_down_hbm,
+    scores_ref,
+    hidden_ref,
+    tails_ref,
     holder_ref,
     slot_ref,
     plen_ref,
@@ -33,16 +53,6 @@
     norm_mlp_ref,
     norm_final_ref,
     w_score_ref,
-    pool_hbm,
-    prompt_hbm,
-    tail_hbm,
-    w_out_hbm,
-    w_gate_hbm,
-    w_up_hbm,
-    w_down_hbm,
-    scores_ref,
-    hidden_ref,
-    tails_ref,
     pool,
     outgoing,
     arrived,
@@ -69,6 +79,8 @@
     page_recv_sem,
     mlp_send_sem,
     mlp_recv_sem,
+    down_send_sem,
+    down_recv_sem,
 ):
     samp = q_ref.shape[2]
     width = res_ref.shape[-1]
@@ -81,6 +93,8 @@
     heads = q_ref.shape[-1] // HEAD
     block = w_out_hbm.shape[0]
     hidden = w_gate_hbm.shape[1]
+    cut = width // 2
+    chunks = down_send.shape[0]
     r = lax.axis_index("req")
     m = lax.axis_index("mlp")
 
@@ -105,15 +119,28 @@
         loads.append(copy)
         return copy
 
+    slot_load = load(slot_hbm, slot_ref)
     pool_load = load(pool_hbm, pool) if exchange else load(pool_hbm, kv.at[1, 0:fetched_rows])
-    prompt_load = load(prompt_hbm, kv.at[0, 0:win])
-    tail_load = load(tail_hbm, kv.at[0, win:fetched_rows])
+    small = [
+        load(holder_hbm, holder_ref),
+        load(plen_hbm, plen_ref),
+        load(tlen_hbm, tlen_ref),
+        load(q_hbm, q_ref),
+        load(new_hbm, new_ref),
+        load(res_hbm, res_ref),
+        load(norm_mlp_hbm, norm_mlp_ref),
+        load(norm_final_hbm, norm_final_ref),
+        load(w_score_hbm, w_score_ref),
+        load(prompt_hbm, kv.at[0, 0:win]),
+        load(tail_hbm, kv.at[0, win:fetched_rows]),
+    ]
     w_out_load = load(w_out_hbm, w_out)
     w_gate_load = load(w_gate_hbm, w_gate)
     w_up_load = load(w_up_hbm, w_up)
     w_down_load = load(w_down_hbm, w_down)
 
     pages = []
+    slot_load.wait()
     if exchange:
         page = pool.shape[1]
         pool_load.wait()
@@ -137,6 +164,8 @@
     else:
         pl.semaphore_wait(barrier, peers)
 
+    for copy in small:
+        copy.wait()
     for i in range(2 * samp):
         q, s = divmod(i, samp)
         qf[2 * i : 2 * i + 2, :] = q_ref[0, q, s].astype(F32)
@@ -196,10 +225,80 @@
             out = jnp.where(line == lead + 1, nf[i + 1 : i + 2, :], out)
             tails_ref[0, q, s] = out.astype(BF16)
 
-    prompt_load.wait()
-    tail_load.wait()
-    first = attend(0)
+    def send_all(source, place, send_sem, recv_sem):
+        copies = []
+        for d in range(1, n_mlp):
+            target = lax.rem(m + d, n_mlp)
+            copy = pltpu.make_async_remote_copy(
+                src_ref=source(target),
+                dst_ref=place(d),
+                send_sem=send_sem(d),
+                recv_sem=recv_sem(d),
+                device_id={"mlp": target},
+                device_id_type=MESH,
+            )
+            copy.start()
+            copies.append(copy)
+        return copies
+
+    def send_phase(phase, q, source, place):
+        return send_all(
+            source,
+            place,
+            lambda d: mlp_send_sem.at[phase, q, d],
+            lambda d: mlp_recv_sem.at[phase, q, d],
+        )
+
+    def fold(x):
+        return jnp.concatenate([x[:, :cut], x[:, cut:]], axis=0).astype(BF16)
+
+    def unfold(x):
+        x = x.astype(F32)
+        return jnp.concatenate([x[:half], x[half:]], axis=1)
+
+    per = block // HEAD
+
+    def send_heads(q, out):
+        for j in range(n_mlp):
+            attn_send[q, j] = jnp.concatenate(
+                [out[(j * per + h) * half : (j * per + h + 1) * half, :] for h in range(per)],
+                axis=1,
+            )
+        copies = send_phase(
+            0, q, lambda t: attn_send.at[q, t], lambda d: attn_recv.at[q, m]
+        )
+        attn_recv[q, m] = attn_send[q, m]
+        return copies
+
+    def project(q, copies):
+        for copy in copies:
+            copy.wait_recv()
+        every = jnp.concatenate([attn_recv[q, j] for j in range(n_mlp)], axis=0).astype(BF16)
+        mixed = jnp.dot(every, w_out[...], preferred_element_type=F32)
+        for j in range(n_mlp):
+            part = mixed[j * half : (j + 1) * half, :]
+            mix_own[q, j] = part
+            mix_send[q, j] = fold(part)
+        return send_phase(1, q, lambda t: mix_send.at[q, t], lambda d: mix_recv.at[q, d])
+
+    def normalise(q, copies):
+        total = rf[q * half : (q + 1) * half, :] + mix_own[q, m]
+        for copy in copies:
+            copy.wait_recv()
+        for d in range(1, n_mlp):
+            total = total + unfold(mix_recv[q, d])
+        h1 = total.astype(BF16).astype(F32)
+        h1_own[q * half : (q + 1) * half, :] = h1
+        scale = lax.rsqrt(jnp.mean(h1 * h1, axis=-1, keepdims=True) + 1e-06)
+        normed[q, m] = fold(h1 * scale * norm_mlp_ref[...].reshape(1, width))
+        return send_phase(2, q, lambda t: normed.at[q, m], lambda d: normed.at[q, m])
+
+    done = []
+    heads_0 = send_heads(0, attend(0))
     write_tails(0)
+    w_out_load.wait()
+    sums_0 = project(0, heads_0)
+    rows_0 = normalise(0, sums_0)
 
     if exchange:
         for copy in pages:
@@ -208,88 +307,65 @@
             kv[1, p * page : (p + 1) * page, :] = arrived[holder_ref[0, p]]
     else:
         pool_load.wait()
-    second = attend(1)
-
-    def pieces(out, j):
-        per = block // HEAD
-        return jnp.concatenate(
-            [out[(j * per + h) * half : (j * per + h + 1) * half, :] for h in range(per)], axis=1
-        )
-
-    for j in range(n_mlp):
-        attn_send[j] = jnp.concatenate([pieces(first, j), pieces(second, j)], axis=0).astype(BF16)
-
-    def send_all(phase, source, place):
-        copies = []
-        for d in range(1, n_mlp):
-            target = lax.rem(m + d, n_mlp)
-            copy = pltpu.make_async_remote_copy(
-                src_ref=source(target),
-                dst_ref=place(d),
-                send_sem=mlp_send_sem.at[phase, d],
-                recv_sem=mlp_recv_sem.at[phase, d],
-                device_id={"mlp": target},
-                device_id_type=MESH,
-            )
-            copy.start()
-            copies.append(copy)
-        return copies
-
-    gathered = send_all(0, lambda t: attn_send.at[t], lambda d: attn_recv.at[m])
-    attn_recv[m] = attn_send[m]
+    heads_1 = send_heads(1, attend(1))
     write_tails(1)
-    w_out_load.wait()
-    for copy in gathered:
-        copy.wait_recv()
-    every = jnp.concatenate([attn_recv[j] for j in range(n_mlp)], axis=0)
-    mixed = jnp.dot(every, w_out[...], preferred_element_type=F32)
-    for j in range(n_mlp):
-        part = mixed[j * rows : (j + 1) * rows, :]
-        mix_own[j] = part
-        mix_send[j] = part.astype(BF16)
-    summed = send_all(1, lambda t: mix_send.at[t], lambda d: mix_recv.at[d])
-    total = rf[...] + mix_own[m]
-    for d in range(1, n_mlp):
-        summed[d - 1].wait_recv()
-        total = total + mix_recv[d].astype(F32)
-    h1 = total.astype(BF16).astype(F32)
-    h1_own[...] = h1
-    scale = lax.rsqrt(jnp.mean(h1 * h1, axis=-1, keepdims=True) + 1e-06)
-    normed[m] = (h1 * scale * norm_mlp_ref[...]).astype(BF16)
-    spread = send_all(2, lambda t: normed.at[m], lambda d: normed.at[m])
+    sums_1 = project(1, heads_1)
     w_gate_load.wait()
     w_up_load.wait()
     w_down_load.wait()
-    for copy in spread:
+    rows_1 = normalise(1, sums_1)
+    for copy in rows_0 + rows_1:
         copy.wait_recv()
-    every = jnp.concatenate([normed[j] for j in range(n_mlp)], axis=0)
-    step = 3 * LANES if hidden % (3 * LANES) == 0 else hidden
+    every = jnp.concatenate(
+        [unfold(normed[q, j]) for j in range(n_mlp) for q in range(2)], axis=0
+    ).astype(BF16)
     acts = []
-    for c in range(0, hidden, step):
-        gate = jnp.dot(every, w_gate[:, c : c + step], preferred_element_type=F32)
-        up = jnp.dot(every, w_up[:, c : c + step], preferred_element_type=F32)
+    for c in range(0, hidden, 2 * LANES):
+        end = min(c + 2 * LANES, hidden)
+        gate = jnp.dot(every, w_gate[:, c:end], preferred_element_type=F32)
+        up = jnp.dot(every, w_up[:, c:end], preferred_element_type=F32)
         acts.append((jax.nn.gelu(gate, approximate=True) * up).astype(BF16))
     act = jnp.concatenate(acts, axis=1)
-    down = jnp.dot(act, w_down[...], preferred_element_type=F32)
-    for j in range(n_mlp):
-        part = down[j * rows : (j + 1) * rows, :]
-        down_own[j] = part
-        down_send[j] = part.astype(BF16)
-    last = send_all(3, lambda t: down_send.at[t], lambda d: down_recv.at[d])
-    h2 = h1_own[...] + down_own[m]
-    for d in range(1, n_mlp):
-        last[d - 1].wait_recv()
-        h2 = h2 + down_recv[d].astype(F32)
+    span = width // chunks
+    last = []
+    for c in range(chunks):
+        down = jnp.dot(act, w_down[:, c * span : (c + 1) * span], preferred_element_type=F32)
+        for j in range(n_mlp):
+            part = down[j * rows : (j + 1) * rows, :]
+            down_own[c, j] = part
+            down_send[c, j] = part.astype(BF16)
+        last.append(
+            send_all(
+                lambda t: down_send.at[c, t],
+                lambda d: down_recv.at[c, d],
+                lambda d: down_send_sem.at[c, d],
+                lambda d: down_recv_sem.at[c, d],
+            )
+        )
+    parts = []
+    for c in range(chunks):
+        part = h1_own[:, c * span : (c + 1) * span] + down_own[c, m]
+        for d in range(1, n_mlp):
+            last[c][d - 1].wait_recv()
+            part = part + down_recv[c, d].astype(F32)
+        parts.append(part)
+    h2 = jnp.concatenate(parts, axis=1)
     scale = lax.rsqrt(jnp.mean(h2 * h2, axis=-1, keepdims=True) + 1e-06)
-    scores_ref[...] = jnp.sum(
-        h2 * scale * norm_final_ref[...] * w_score_ref[...], axis=-1, keepdims=True
-    )
+    gain = (norm_final_ref[...] * w_score_ref[...]).reshape(1, width)
+    sums = jnp.sum(h2 * scale * gain, axis=-1, keepdims=True)
+    col = lax.broadcasted_iota(jnp.int32, (rows, 2), 1)
+    line = lax.broadcasted_iota(jnp.int32, (rows, 2), 0)
+    paired = jnp.where(line % 2 == col, sums, 0.0)
     rf[...] = h2
     for i in range(2 * samp):
         q, s = divmod(i, samp)
         hidden_ref[0, q, s] = rf[2 * i : 2 * i + 2, :].astype(BF16)
-    for copy in pages + gathered + summed + spread + last:
-        copy.wait_send()
+        scores_ref[0, q, s : s + 1, :] = jnp.sum(
+            paired[2 * i : 2 * i + 2, :], axis=0, keepdims=True
+        )
+    for group in [pages, heads_0, sums_0, rows_0, heads_1, sums_1, rows_1] + last:
+        for copy in group:
+            copy.wait_send()
 
 
 def on_device(
@@ -334,19 +410,29 @@
         page_bufs = (1, 16, kv_width)
     pool_buf = page_pool.shape if exchange else page_bufs
     vmem = pl.BlockSpec(memory_space=pltpu.VMEM)
-    smem = pl.BlockSpec(memory_space=pltpu.SMEM)
-    hbm = pl.BlockSpec(memory_space=pl.ANY)
+    hbm = pl.BlockSpec(memory_space=pltpu.HBM)
     sems = n_req if exchange else 1
+    chunks = 3
     scores, hidden_out, tails_out = pl.pallas_call(
         functools.partial(block_kernel, n_req, n_mlp, exchange),
         out_shape=(
-            jax.ShapeDtypeStruct((rows, 1), F32),
+            jax.ShapeDtypeStruct((1, 2, samp, 2), F32),
             jax.ShapeDtypeStruct(residual.shape, BF16),
             jax.ShapeDtypeStruct((1, 2, samp, tail_rows, kv_width), BF16),
         ),
-        in_specs=[smem] * 4 + [vmem] * 6 + [hbm] * 7,
+        in_specs=[hbm] * 17,
         out_specs=(vmem, vmem, vmem),
         scratch_shapes=[
+            pltpu.SMEM(page_holder.shape, jnp.int32),
+            pltpu.SMEM(serve_slot.shape, jnp.int32),
+            pltpu.SMEM(prompt_len.shape, jnp.int32),
+            pltpu.SMEM(tail_len.shape, jnp.int32),
+            pltpu.VMEM(queries.shape, BF16),
+            pltpu.VMEM(new_kv.shape, BF16),
+            pltpu.VMEM(residual.shape, BF16),
+            pltpu.VMEM(norm_mlp.shape, F32),
+            pltpu.VMEM(norm_final.shape, F32),
+            pltpu.VMEM(w_score.shape, F32),
             pltpu.VMEM(pool_buf, BF16),
             pltpu.VMEM(page_bufs, BF16),
             pltpu.VMEM(page_bufs, BF16),
@@ -358,21 +444,23 @@
             pltpu.VMEM((rows, queries.shape[-1]), F32),
             pltpu.VMEM((rows, kv_width), F32),
             pltpu.VMEM((rows, width), F32),
-            pltpu.VMEM((n_mlp, rows, block), BF16),
-            pltpu.VMEM((n_mlp, rows, block), BF16),
-            pltpu.VMEM((n_mlp, rows, width), F32),
-            pltpu.VMEM((n_mlp, rows, width), BF16),
-            pltpu.VMEM((n_mlp, rows, width), BF16),
-            pltpu.VMEM((n_mlp, rows, width), BF16),
-            pltpu.VMEM((n_mlp, rows, width), F32),
-            pltpu.VMEM((n_mlp, rows, width), BF16),
-            pltpu.VMEM((n_mlp, rows, width), BF16),
+            pltpu.VMEM((2, n_mlp, rows // 2, block), F32),
+            pltpu.VMEM((2, n_mlp, rows // 2, block), F32),
+            pltpu.VMEM((2, n_mlp, rows // 2, width), F32),
+            pltpu.VMEM((2, n_mlp, rows, width // 2), BF16),
+            pltpu.VMEM((2, n_mlp, rows, width // 2), BF16),
+            pltpu.VMEM((2, n_mlp, rows, width // 2), BF16),
+            pltpu.VMEM((chunks, n_mlp, rows, width // chunks), F32),
+            pltpu.VMEM((chunks, n_mlp, rows, width // chunks), BF16),
+            pltpu.VMEM((chunks, n_mlp, rows, width // chunks), BF16),
             pltpu.VMEM((rows, width), F32),
-            pltpu.SemaphoreType.DMA((7,)),
+            pltpu.SemaphoreType.DMA((17,)),
             pltpu.SemaphoreType.DMA((sems,)),
             pltpu.SemaphoreType.DMA((sems,)),
-            pltpu.SemaphoreType.DMA((4, n_mlp)),
-            pltpu.SemaphoreType.DMA((4, n_mlp)),
+            pltpu.SemaphoreType.DMA((3, 2, n_mlp)),
+            pltpu.SemaphoreType.DMA((3, 2, n_mlp)),
+            pltpu.SemaphoreType.DMA((chunks, n_mlp)),
+            pltpu.SemaphoreType.DMA((chunks, n_mlp)),
         ],
         compiler_params=pltpu.CompilerParams(
             collective_id=0, has_side_effects=True, vmem_limit_bytes=48 * 1024 * 1024
@@ -390,9 +478,9 @@
         queries,
         new_kv,
         residual,
-        norm_mlp.reshape(1, -1),
-        norm_final.reshape(1, -1),
-        w_score.reshape(1, -1),
+        norm_mlp,
+        norm_final,
+        w_score,
         pool,
         prompt_kv.reshape(win, kv_width),
         tail_kv.reshape(samp * tail_rows, kv_width),
@@ -401,7 +489,7 @@
         w_up,
         w_down,
     )
-    return scores.reshape(1, 2, samp, 2), hidden_out, tails_out
+    return scores, hidden_out, tails_out
 
 
 def solution(mesh):

time: 51.9 us -> 49.8 us (0.960)
  Pallas kernels: 36.9 us -> 35.2 us
    reshape x4 -> x0, local copies, waits for them, and re-layouts: 2.19 us -> none  [the longest x1 0.7 us: on_device(): norm_mlp.reshape(1, -1)]
    pallas_call x1, Pallas kernels: 36.9 us -> 35.2 us  [on_device(): pl.pallas_call(functools.partial(block_kernel, n_req, n_mlp, exchange), o...]
    unnamed x25 -> x30, local copies, waits for them, and re-layouts: 11.2 us -> 12.6 us
    pallas_call x0 -> x1, local copies, waits for them, and re-layouts: none -> 0.67 us  [on_device(): pl.pallas_call(functools.partial(block_kernel, n_req, n_mlp, exchange), o...]
where the time goes in v2:
time: 49.8 us; the launch traced here: 49.2 us
  Pallas kernels  35.2 us (71%)
  local copies, waits for them, and re-layouts  13.3 us (27%)
  between operations  0.67 us (1%)
    pallas_call x1, Pallas kernels, on_device(): pl.pallas_call(functools.partial(block_kernel, n_req, n_mlp, exchange), o...  35.2 us
    unnamed x30, local copies, waits for them, and re-layouts  12.6 us

profile of v2, /device:TPU:0, one launch (start us, length us, event | category | flops | bytes accessed | tf_op | source)
XLA Modules:
  0.0 49.2 jit_solution(16541636806074750921)
XLA Ops:
  0.6 0.0 copy-start
  0.6 1.3 %copy-done = bf16[384,1536]{1,0:T(8,128)(2,1)S(1)} copy-done((bf16[384,1536]{1,0:T(8,128)(2,1)S(1)}, bf16[384,1536]{1,0:T(8,128)(2,1)}, u32[]{:S(2)}) %copy-start) | copy-done | bytes 1179672
  1.9 0.0 copy-start.1
  1.9 1.1 %copy-done.1 = bf16[8,160,256]{2,1,0:T(8,128)(2,1)S(1)} copy-done((bf16[8,160,256]{2,1,0:T(8,128)(2,1)S(1)}, bf16[8,160,256]{2,1,0:T(8,128)(2,1)}, u32[]{:S(2)}) %copy-start.1) | copy-done | bytes 655384
  3.0 0.0 copy-start.2
  3.0 1.0 %copy-done.2 = bf16[1,1024,256]{2,1,0:T(8,128)(2,1)S(1)} copy-done((bf16[1,1024,256]{2,1,0:T(8,128)(2,1)S(1)}, bf16[1,1024,256]{2,1,0:T(8,128)(2,1)}, u32[]{:S(2)}) %copy-start.2) | copy-done | bytes 524312
  4.0 0.0 copy-start.3
  4.0 0.9 %copy-done.3 = bf16[1,4,64,256]{3,2,1,0:T(8,128)(2,1)S(1)} copy-done((bf16[1,4,64,256]{3,2,1,0:T(8,128)(2,1)S(1)}, bf16[1,4,64,256]{3,2,1,0:T(8,128)(2,1)}, u32[]{:S(2)}) %copy-start.3) | copy-done | bytes 131096
  4.9 0.0 copy-start.4
  4.9 0.8 %copy-done.4 = bf16[1,2,4,2,1536]{4,3,2,1,0:T(2,128)(2,1)S(1)} copy-done((bf16[1,2,4,2,1536]{4,3,2,1,0:T(2,128)(2,1)S(1)}, bf16[1,2,4,2,1536]{4,3,2,1,0:T(2,128)(2,1)}, u32[]{:S(2)}) %copy-start.4) | copy-done | bytes 49176
  5.7 0.0 copy-start.5
  5.7 0.8 %copy-done.5 = bf16[1,2,4,2,1536]{4,3,2,1,0:T(2,128)(2,1)S(1)} copy-done((bf16[1,2,4,2,1536]{4,3,2,1,0:T(2,128)(2,1)S(1)}, bf16[1,2,4,2,1536]{4,3,2,1,0:T(2,128)(2,1)}, u32[]{:S(2)}) %copy-start.5) | copy-done | bytes 49176
  6.5 0.0 copy-start.6
  6.5 0.7 %copy-done.6 = bf16[1,2,4,2,256]{4,3,2,1,0:T(2,128)(2,1)S(1)} copy-done((bf16[1,2,4,2,256]{4,3,2,1,0:T(2,128)(2,1)S(1)}, bf16[1,2,4,2,256]{4,3,2,1,0:T(2,128)(2,1)}, u32[]{:S(2)}) %copy-start.6) | copy-done | bytes 8216
  7.2 0.0 copy-start.7
  7.2 0.7 %copy-done.7 = f32[1536]{0:T(1024)S(1)} copy-done((f32[1536]{0:T(1024)S(1)}, f32[1536]{0:T(1024)}, u32[]{:S(2)}) %copy-start.7) | copy-done | bytes 6168
  7.9 0.0 copy-start.8
  7.9 0.7 %copy-done.8 = f32[1536]{0:T(1024)S(1)} copy-done((f32[1536]{0:T(1024)S(1)}, f32[1536]{0:T(1024)}, u32[]{:S(2)}) %copy-start.8) | copy-done | bytes 6168
  8.6 0.0 copy-start.9
  8.6 0.7 %copy-done.9 = f32[1536]{0:T(1024)S(1)} copy-done((f32[1536]{0:T(1024)S(1)}, f32[1536]{0:T(1024)}, u32[]{:S(2)}) %copy-start.9) | copy-done | bytes 6168
  9.3 0.0 copy-start.10
  9.3 0.7 %copy-done.10 = s32[1,2,4]{2,1,0:T(2,128)S(1)} copy-done((s32[1,2,4]{2,1,0:T(2,128)S(1)}, s32[1,2,4]{2,1,0:T(2,128)}, u32[]{:S(2)}) %copy-start.10) | copy-done | bytes 56
  10.0 0.0 copy-start.11
  10.0 0.7 %copy-done.11 = s32[1,8]{1,0:T(1,128)S(1)} copy-done((s32[1,8]{1,0:T(1,128)S(1)}, s32[1,8]{1,0:T(1,128)}, u32[]{:S(2)}) %copy-start.11) | copy-done | bytes 56
  10.7 0.0 copy-start.12
  10.7 0.7 %copy-done.12 = s32[1,8]{1,0:T(1,128)S(1)} copy-done((s32[1,8]{1,0:T(1,128)S(1)}, s32[1,8]{1,0:T(1,128)}, u32[]{:S(2)}) %copy-start.12) | copy-done | bytes 56
  11.3 0.0 copy-start.13
  11.3 0.7 %copy-done.13 = s32[1,2]{1,0:T(1,128)S(1)} copy-done((s32[1,2]{1,0:T(1,128)S(1)}, s32[1,2]{1,0:T(1,128)}, u32[]{:S(2)}) %copy-start.13) | copy-done | bytes 32
  12.0 35.2 %shard_map.184 = (f32[1,2,4,2]{3,2,1,0:T(4,128)S(1)}, bf16[1,2,4,2,1536]{4,3,2,1,0:T(2,128)(2,1)S(1)}, bf16[1,2,4,64,256]{4,3,2,1,0:T(8,128)(2,1)S(1)}) custom-call(s32[1,8]{1,0:T(1,128)S(1)} %copy-done.11, s32[1,8]{1,0:T(1,128)S(1)} %copy-done.12, s32[1,2]{1,0:T(1,128)S(1)} %copy-done.13, s32[1,2,4]{2,1,0:T(2,128)S(1)} %copy-done.10, ...), custom_call_target="tpu_custom_call" | custom-call | flops 754974720 | bytes 11796480 | tf_op jit(solution)/shard_map/pallas_call | solution.py:416
  47.2 0.7 %copy.20 = f32[1,2,4,2]{2,3,1,0:T(2,128)} copy(f32[1,2,4,2]{3,2,1,0:T(4,128)S(1)} %get-tuple-element.3) | data formatting | bytes 128 | tf_op jit(solution)/shard_map/pallas_call | solution.py:416
  47.8 0.6 %copy.23 = bf16[1,2,4,2,1536]{4,3,2,1,0:T(2,128)(2,1)} copy(bf16[1,2,4,2,1536]{4,3,2,1,0:T(2,128)(2,1)S(1)} %get-tuple-element.10) | data formatting | bytes 98304
  48.5 0.7 %copy.24 = bf16[1,2,4,64,256]{4,3,2,1,0:T(8,128)(2,1)} copy(bf16[1,2,4,64,256]{4,3,2,1,0:T(8,128)(2,1)S(1)} %get-tuple-element.11) | data formatting | bytes 524288
Async XLA Ops:
  0.6 1.3 %copy-start = (bf16[384,1536]{1,0:T(8,128)(2,1)S(1)}, bf16[384,1536]{1,0:T(8,128)(2,1)}, u32[]{:S(2)}) copy-start(bf16[384,1536]{1,0:T(8,128)(2,1)} %w_out_hbm.1) | copy-start | bytes 3538948
  1.9 1.1 %copy-start.1 = (bf16[8,160,256]{2,1,0:T(8,128)(2,1)S(1)}, bf16[8,160,256]{2,1,0:T(8,128)(2,1)}, u32[]{:S(2)}) copy-start(bf16[8,160,256]{2,1,0:T(8,128)(2,1)} %pool_hbm.1) | copy-start | bytes 1966084
  3.0 1.0 %copy-start.2 = (bf16[1,1024,256]{2,1,0:T(8,128)(2,1)S(1)}, bf16[1,1024,256]{2,1,0:T(8,128)(2,1)}, u32[]{:S(2)}) copy-start(bf16[1,1024,256]{2,1,0:T(8,128)(2,1)} %param.20) | copy-start | bytes 1572868
  4.0 0.9 %copy-start.3 = (bf16[1,4,64,256]{3,2,1,0:T(8,128)(2,1)S(1)}, bf16[1,4,64,256]{3,2,1,0:T(8,128)(2,1)}, u32[]{:S(2)}) copy-start(bf16[1,4,64,256]{3,2,1,0:T(8,128)(2,1)} %param.21) | copy-start | bytes 393220
  4.9 0.8 %copy-start.4 = (bf16[1,2,4,2,1536]{4,3,2,1,0:T(2,128)(2,1)S(1)}, bf16[1,2,4,2,1536]{4,3,2,1,0:T(2,128)(2,1)}, u32[]{:S(2)}) copy-start(bf16[1,2,4,2,1536]{4,3,2,1,0:T(2,128)(2,1)} %q_hbm.1) | copy-start | bytes 147460
  5.7 0.8 %copy-start.5 = (bf16[1,2,4,2,1536]{4,3,2,1,0:T(2,128)(2,1)S(1)}, bf16[1,2,4,2,1536]{4,3,2,1,0:T(2,128)(2,1)}, u32[]{:S(2)}) copy-start(bf16[1,2,4,2,1536]{4,3,2,1,0:T(2,128)(2,1)} %res_hbm.1) | copy-start | bytes 147460
  6.5 0.7 %copy-start.6 = (bf16[1,2,4,2,256]{4,3,2,1,0:T(2,128)(2,1)S(1)}, bf16[1,2,4,2,256]{4,3,2,1,0:T(2,128)(2,1)}, u32[]{:S(2)}) copy-start(bf16[1,2,4,2,256]{4,3,2,1,0:T(2,128)(2,1)} %new_hbm.1) | copy-start | bytes 24580
  7.2 0.7 %copy-start.7 = (f32[1536]{0:T(1024)S(1)}, f32[1536]{0:T(1024)}, u32[]{:S(2)}) copy-start(f32[1536]{0:T(1024)} %norm_mlp_hbm.1) | copy-start | bytes 18436
  7.9 0.7 %copy-start.8 = (f32[1536]{0:T(1024)S(1)}, f32[1536]{0:T(1024)}, u32[]{:S(2)}) copy-start(f32[1536]{0:T(1024)} %norm_final_hbm.1) | copy-start | bytes 18436
  8.6 0.7 %copy-start.9 = (f32[1536]{0:T(1024)S(1)}, f32[1536]{0:T(1024)}, u32[]{:S(2)}) copy-start(f32[1536]{0:T(1024)} %w_score_hbm.1) | copy-start | bytes 18436
  9.3 0.7 %copy-start.10 = (s32[1,2,4]{2,1,0:T(2,128)S(1)}, s32[1,2,4]{2,1,0:T(2,128)}, u32[]{:S(2)}) copy-start(s32[1,2,4]{2,1,0:T(2,128)} %tlen_hbm.1) | copy-start | bytes 100
  10.0 0.7 %copy-start.11 = (s32[1,8]{1,0:T(1,128)S(1)}, s32[1,8]{1,0:T(1,128)}, u32[]{:S(2)}) copy-start(s32[1,8]{1,0:T(1,128)} %holder_hbm.1) | copy-start | bytes 100
  10.7 0.7 %copy-start.12 = (s32[1,8]{1,0:T(1,128)S(1)}, s32[1,8]{1,0:T(1,128)}, u32[]{:S(2)}) copy-start(s32[1,8]{1,0:T(1,128)} %slot_hbm.1) | copy-start | bytes 100
  11.3 0.7 %copy-start.13 = (s32[1,2]{1,0:T(1,128)S(1)}, s32[1,2]{1,0:T(1,128)}, u32[]{:S(2)}) copy-start(s32[1,2]{1,0:T(1,128)} %plen_hbm.1) | copy-start | bytes 28

commit v3 on v2

--- a/solution.py
+++ b/solution.py
@@ -40,6 +40,9 @@
     w_gate_hbm,
     w_up_hbm,
     w_down_hbm,
+    scores_hbm,
+    hidden_hbm,
+    tails_hbm,
     scores_ref,
     hidden_ref,
     tails_ref,
@@ -81,6 +84,7 @@
     mlp_recv_sem,
     down_send_sem,
     down_recv_sem,
+    store_sem,
 ):
     samp = q_ref.shape[2]
     width = res_ref.shape[-1]
@@ -224,6 +228,9 @@
             out = jnp.where(line == lead, nf[i : i + 1, :], old)
             out = jnp.where(line == lead + 1, nf[i + 1 : i + 2, :], out)
             tails_ref[0, q, s] = out.astype(BF16)
+        copy = pltpu.make_async_copy(tails_ref.at[0, q], tails_hbm.at[0, q], store_sem.at[q])
+        copy.start()
+        return copy
 
     def send_all(source, place, send_sem, recv_sem):
         copies = []
@@ -295,7 +302,7 @@
 
     done = []
     heads_0 = send_heads(0, attend(0))
-    write_tails(0)
+    stores = [write_tails(0)]
     w_out_load.wait()
     sums_0 = project(0, heads_0)
     rows_0 = normalise(0, sums_0)
@@ -308,7 +315,7 @@
     else:
         pool_load.wait()
     heads_1 = send_heads(1, attend(1))
-    write_tails(1)
+    stores.append(write_tails(1))
     sums_1 = project(1, heads_1)
     w_gate_load.wait()
     w_up_load.wait()
@@ -350,22 +357,40 @@
             part = part + down_recv[c, d].astype(F32)
         parts.append(part)
     h2 = jnp.concatenate(parts, axis=1)
-    scale = lax.rsqrt(jnp.mean(h2 * h2, axis=-1, keepdims=True) + 1e-06)
-    gain = (norm_final_ref[...] * w_score_ref[...]).reshape(1, width)
-    sums = jnp.sum(h2 * scale * gain, axis=-1, keepdims=True)
-    col = lax.broadcasted_iota(jnp.int32, (rows, 2), 1)
-    line = lax.broadcasted_iota(jnp.int32, (rows, 2), 0)
-    paired = jnp.where(line % 2 == col, sums, 0.0)
     rf[...] = h2
     for i in range(2 * samp):
         q, s = divmod(i, samp)
         hidden_ref[0, q, s] = rf[2 * i : 2 * i + 2, :].astype(BF16)
-        scores_ref[0, q, s : s + 1, :] = jnp.sum(
-            paired[2 * i : 2 * i + 2, :], axis=0, keepdims=True
-        )
+    copy = pltpu.make_async_copy(hidden_ref, hidden_hbm, store_sem.at[2])
+    copy.start()
+    stores.append(copy)
+    scale = lax.rsqrt(jnp.mean(h2 * h2, axis=-1, keepdims=True) + 1e-06)
+    gain = (norm_final_ref[...] * w_score_ref[...]).reshape(1, width)
+    sums = jnp.sum(h2 * scale * gain, axis=-1, keepdims=True)
+    col = lax.broadcasted_iota(jnp.int32, (half, samp), 1)
+    line = lax.broadcasted_iota(jnp.int32, (half, samp), 0)
+    for q in range(2):
+        for t in range(2):
+            picked = jnp.where(line == 2 * col + t, sums[q * half : (q + 1) * half, :], 0.0)
+            scores_ref[0, q, t : t + 1, :] = jnp.sum(picked, axis=0, keepdims=True)
+    copy = pltpu.make_async_copy(scores_ref, scores_hbm, store_sem.at[3])
+    copy.start()
+    stores.append(copy)
     for group in [pages, heads_0, sums_0, rows_0, heads_1, sums_1, rows_1] + last:
         for copy in group:
             copy.wait_send()
+    for copy in stores:
+        copy.wait()
+
+
+def hand_over(*refs):
+    count = (len(refs) - 1) // 2
+    sem = refs[-1]
+    copies = [pltpu.make_async_copy(refs[i], refs[count + i], sem.at[i]) for i in range(count)]
+    for copy in copies:
+        copy.start()
+    for copy in copies:
+        copy.wait()
 
 
 def on_device(
@@ -409,20 +434,22 @@
         pool = jnp.take(arrived, page_holder[0], axis=0).reshape(-1, kv_width)
         page_bufs = (1, 16, kv_width)
     pool_buf = page_pool.shape if exchange else page_bufs
-    vmem = pl.BlockSpec(memory_space=pltpu.VMEM)
     hbm = pl.BlockSpec(memory_space=pltpu.HBM)
     sems = n_req if exchange else 1
     chunks = 3
-    scores, hidden_out, tails_out = pl.pallas_call(
+    made = pl.pallas_call(
         functools.partial(block_kernel, n_req, n_mlp, exchange),
         out_shape=(
-            jax.ShapeDtypeStruct((1, 2, samp, 2), F32),
+            jax.ShapeDtypeStruct((1, 2, 2, samp), F32),
             jax.ShapeDtypeStruct(residual.shape, BF16),
             jax.ShapeDtypeStruct((1, 2, samp, tail_rows, kv_width), BF16),
         ),
         in_specs=[hbm] * 17,
-        out_specs=(vmem, vmem, vmem),
+        out_specs=(hbm, hbm, hbm),
         scratch_shapes=[
+            pltpu.VMEM((1, 2, 2, samp), F32),
+            pltpu.VMEM(residual.shape, BF16),
+            pltpu.VMEM((1, 2, samp, tail_rows, kv_width), BF16),
             pltpu.SMEM(page_holder.shape, jnp.int32),
             pltpu.SMEM(serve_slot.shape, jnp.int32),
             pltpu.SMEM(prompt_len.shape, jnp.int32),
@@ -461,9 +488,10 @@
             pltpu.SemaphoreType.DMA((3, 2, n_mlp)),
             pltpu.SemaphoreType.DMA((chunks, n_mlp)),
             pltpu.SemaphoreType.DMA((chunks, n_mlp)),
+            pltpu.SemaphoreType.DMA((4,)),
         ],
         compiler_params=pltpu.CompilerParams(
-            collective_id=0, has_side_effects=True, vmem_limit_bytes=48 * 1024 * 1024
+            collective_id=0, has_side_effects=True, vmem_limit_bytes=60 * 1024 * 1024
         ),
         cost_estimate=pl.CostEstimate(
             flops=2 * n_mlp * rows * width * (block + 3 * hidden),
@@ -489,7 +517,15 @@
         w_up,
         w_down,
     )
-    return scores, hidden_out, tails_out
+    scores, hidden_out, tails_out = pl.pallas_call(
+        hand_over,
+        out_shape=tuple(jax.ShapeDtypeStruct(x.shape, x.dtype) for x in made),
+        in_specs=[hbm] * 3,
+        out_specs=(hbm,) * 3,
+        scratch_shapes=[pltpu.SemaphoreType.DMA((3,))],
+        compiler_params=pltpu.CompilerParams(vmem_limit_bytes=60 * 1024 * 1024),
+    )(*made)
+    return jnp.swapaxes(scores, 2, 3), hidden_out, tails_out
 
 
 def solution(mesh):

time: 49.8 us -> 47.2 us (0.948)
  local copies, waits for them, and re-layouts: 13.3 us -> 0 us
  Pallas kernels: 35.2 us -> 46.4 us
    unnamed x30 -> x0, local copies, waits for them, and re-layouts: 12.6 us -> none
    pallas_call x0 -> x1, Pallas kernels: none -> 10.6 us  [on_device(): pl.pallas_call(hand_over, out_shape=tuple((jax.ShapeDtypeStruct(x.shape,...]
    pallas_call x1 -> x0, local copies, waits for them, and re-layouts: 0.67 us -> none  [on_device(): pl.pallas_call(functools.partial(block_kernel, n_req, n_mlp, exchange), o...]
    pallas_call x1, Pallas kernels: 35.2 us -> 35.8 us  [on_device(): pl.pallas_call(functools.partial(block_kernel, n_req, n_mlp, exchange), o...]
where the time goes in v3:
time: 47.2 us; the launch traced here: 47 us
  Pallas kernels  46.4 us (98%)
  between operations  0.65 us (1%)
    pallas_call x1, Pallas kernels, on_device(): pl.pallas_call(functools.partial(block_kernel, n_req, n_mlp, exchange), o...  35.8 us
    pallas_call x1, Pallas kernels, on_device(): pl.pallas_call(hand_over, out_shape=tuple((jax.ShapeDtypeStruct(x.shape,...  10.6 us

profile of v3, /device:TPU:0, one launch (start us, length us, event | category | flops | bytes accessed | tf_op | source)
XLA Modules:
  0.0 47.0 jit_solution(6309449712423478970)
XLA Ops:
  0.6 35.8 %shard_map.184 = (f32[1,2,2,4]{3,2,1,0:T(2,128)}, bf16[1,2,4,2,1536]{4,3,2,1,0:T(2,128)(2,1)}, bf16[1,2,4,64,256]{4,3,2,1,0:T(8,128)(2,1)}) custom-call(s32[1,8]{1,0:T(1,128)} %holder_hbm.1, s32[1,8]{1,0:T(1,128)} %slot_hbm.1, s32[1,2]{1,0:T(1,128)} %plen_hbm.1, s32[1,2,4]{2,1,0:T(2,128)} %tlen_hbm.1, bf16[1,2,4,2,1536]{4,3,2,1,0:T(2,128)(2,1)} %q_hbm.1, ...), custom_call_target="tpu_custom_call" | custom-call | flops 754974720 | bytes 11796480 | tf_op jit(solution)/shard_map/pallas_call | solution.py:440
  36.4 10.6 %shard_map.185 = (f32[1,2,2,4]{3,2,1,0:T(2,128)}, bf16[1,2,4,2,1536]{4,3,2,1,0:T(2,128)(2,1)}, bf16[1,2,4,64,256]{4,3,2,1,0:T(8,128)(2,1)}) custom-call(f32[1,2,2,4]{3,2,1,0:T(2,128)} %get-tuple-element.9.refs_0_, bf16[1,2,4,2,1536]{4,3,2,1,0:T(2,128)(2,1)} %get-tuple-element.10.refs_1_, bf16[1,2,4,64,256]{4,3,2,1,0:T(8,128)(2,1)} %get-tuple-element.11.refs_2_), custom_call_target="tpu_custom_call" | custom-call | tf_op jit(solution)/shard_map/pallas_call | solution.py:520

commit v4 on v3

--- a/solution.py
+++ b/solution.py
@@ -384,12 +384,17 @@
 
 
 def hand_over(*refs):
-    count = (len(refs) - 1) // 2
-    sem = refs[-1]
-    copies = [pltpu.make_async_copy(refs[i], refs[count + i], sem.at[i]) for i in range(count)]
-    for copy in copies:
+    count = (len(refs) - 2) // 3
+    made, out, held = refs[:count], refs[count : 2 * count], refs[2 * count : 3 * count]
+    in_sem, out_sem = refs[-2], refs[-1]
+    ins = [pltpu.make_async_copy(made[i], held[i], in_sem.at[i]) for i in range(count)]
+    outs = [pltpu.make_async_copy(held[i], out[i], out_sem.at[i]) for i in range(count)]
+    for copy in ins:
         copy.start()
-    for copy in copies:
+    for i in range(count):
+        ins[i].wait()
+        outs[i].start()
+    for copy in outs:
         copy.wait()
 
 
@@ -522,7 +527,8 @@
         out_shape=tuple(jax.ShapeDtypeStruct(x.shape, x.dtype) for x in made),
         in_specs=[hbm] * 3,
         out_specs=(hbm,) * 3,
-        scratch_shapes=[pltpu.SemaphoreType.DMA((3,))],
+        scratch_shapes=[pltpu.VMEM(x.shape, x.dtype) for x in made]
+        + [pltpu.SemaphoreType.DMA((3,)), pltpu.SemaphoreType.DMA((3,))],
         compiler_params=pltpu.CompilerParams(vmem_limit_bytes=60 * 1024 * 1024),
     )(*made)
     return jnp.swapaxes(scores, 2, 3), hidden_out, tails_out

time: 47.2 us -> 38.3 us (0.81)
  Pallas kernels: 46.4 us -> 37.5 us
    pallas_call x1, Pallas kernels: 10.6 us -> 1.74 us  [on_device(): pl.pallas_call(hand_over, out_shape=tuple((jax.ShapeDtypeStruct(x.shape,...]
where the time goes in v4:
time: 38.3 us; the launch traced here: 38.2 us
  Pallas kernels  37.5 us (98%)
  between operations  0.65 us (2%)
    pallas_call x1, Pallas kernels, on_device(): pl.pallas_call(functools.partial(block_kernel, n_req, n_mlp, exchange), o...  35.8 us
    pallas_call x1, Pallas kernels, on_device(): pl.pallas_call(hand_over, out_shape=tuple((jax.ShapeDtypeStruct(x.shape,...  1.74 us

profile of v4, /device:TPU:0, one launch (start us, length us, event | category | flops | bytes accessed | tf_op | source)
XLA Modules:
  0.0 38.2 jit_solution(14335355328994409121)
XLA Ops:
  0.6 35.8 %shard_map.184 = (f32[1,2,2,4]{3,2,1,0:T(2,128)}, bf16[1,2,4,2,1536]{4,3,2,1,0:T(2,128)(2,1)}, bf16[1,2,4,64,256]{4,3,2,1,0:T(8,128)(2,1)}) custom-call(s32[1,8]{1,0:T(1,128)} %holder_hbm.1, s32[1,8]{1,0:T(1,128)} %slot_hbm.1, s32[1,2]{1,0:T(1,128)} %plen_hbm.1, s32[1,2,4]{2,1,0:T(2,128)} %tlen_hbm.1, bf16[1,2,4,2,1536]{4,3,2,1,0:T(2,128)(2,1)} %q_hbm.1, ...), custom_call_target="tpu_custom_call" | custom-call | flops 754974720 | bytes 11796480 | tf_op jit(solution)/shard_map/pallas_call | solution.py:445
  36.4 1.7 %shard_map.185 = (f32[1,2,2,4]{3,2,1,0:T(2,128)}, bf16[1,2,4,2,1536]{4,3,2,1,0:T(2,128)(2,1)}, bf16[1,2,4,64,256]{4,3,2,1,0:T(8,128)(2,1)}) custom-call(f32[1,2,2,4]{3,2,1,0:T(2,128)} %get-tuple-element.9.refs_0_, bf16[1,2,4,2,1536]{4,3,2,1,0:T(2,128)(2,1)} %get-tuple-element.10.refs_1_, bf16[1,2,4,64,256]{4,3,2,1,0:T(8,128)(2,1)} %get-tuple-element.11.refs_2_), custom_call_target="tpu_custom_call" | custom-call | tf_op jit(solution)/shard_map/pallas_call | solution.py:525
